TPU v7x, 128 devices: a whole 4x4x4 slice. The times are simulated.
128 devices in a mesh: agent: 16 (over x_hi, z, core), seq: 8 (over y, x_lo).
Axes of the slice: x: 4 (x_hi: 2, x_lo: 2; x = x_hi * 2 + x_lo), y: 4, z: 4, core: 2. Of those that a mesh axis runs over, the one named last changes fastest.
Arguments:
- queries: bfloat16 [16, 1024, 1024], P('agent', 'seq'), may hold values from -8 to 8
- key_codes: bfloat16 [16, 1024, 1024], P('agent', 'seq'), may hold values from -8 to 8
- key_exps: int32 [16, 8, 8], P('agent', 'seq'), may hold values from -1 to 1
- value_codes: bfloat16 [16, 1024, 1024], P('agent', 'seq'), may hold values from -6 to 6
- value_exps: int32 [16, 8, 8], P('agent', 'seq'), may hold values from -1 to 1
- d_out: bfloat16 [16, 1024, 2048], P('agent', 'seq'), may hold values from -6 to 6
- out_weight: float32 [16, 1024, 2048], P('agent', 'seq'), may hold values from -0.1875 to 0.1875
- prev_psi: float32 [16, 1024, 2048], P('agent', 'seq'), may hold values from -0.1875 to 0.1875
- mixing: int32 [16, 2], P('agent'), may hold values from 1 to 4, as said below
Outputs:
- d_queries: bfloat16 [16, 1024, 1024], P('agent', 'seq')
- d_keys: bfloat16 [16, 1024, 1024], P('agent', 'seq')
- d_values: bfloat16 [16, 1024, 1024], P('agent', 'seq')
- new_weight: float32 [16, 1024, 2048], P('agent', 'seq')
- new_psi: float32 [16, 1024, 2048], P('agent', 'seq')
Inputs may be any that keep to these rules, and one draw needn't show every extreme that they name: mixing[a, 1] equals mixing[a + 1, 0] with agent indices modulo 16: one numerator for each edge of the loop, so that the mixing matrix is symmetric and doubly stochastic with an own weight of one half or more; in every draw some edge has the numerator 1 and some edge 4.
All inputs are finite; a program needn't handle non-finite values.
Results may differ from a plain program's by a relative error of at most 0.035.
Values may be sent and summed in bfloat16 or wider, within the bound.
A program may use at most 128 MiB of HBM per device.

v0:
```python
import jax
import jax.numpy as jnp
from jax import lax
from jax.sharding import PartitionSpec as P

HEADS = 8
HDIM = 128
SBLK = 128


def with_halo(cells, sides, width):
    for axis, dim in sides:
        count = lax.axis_size(axis)
        head = lax.slice_in_dim(cells, 0, width, axis=dim)
        tail = lax.slice_in_dim(cells, cells.shape[dim] - width, cells.shape[dim], axis=dim)
        cells = jnp.concatenate(
            [
                lax.ppermute(tail, axis, [(i, (i + 1) % count) for i in range(count)]),
                cells,
                lax.ppermute(head, axis, [((i + 1) % count, i) for i in range(count)]),
            ],
            axis=dim,
        )
    return cells


def dequant(code, expo):
    factor = jnp.exp2(expo.astype(jnp.float32))
    blocks = (
        code.astype(jnp.float32).reshape(expo.shape[0], SBLK, HEADS, HDIM)
        * factor[:, None, :, None]
    )
    return blocks.reshape(code.shape).astype(jnp.bfloat16)


def inner(left, right):
    return lax.dot_general(
        left, right, (((1,), (1,)), ((), ())), preferred_element_type=jnp.float32
    )


def across(left, right):
    return lax.dot_general(
        left, right, (((0,), (0,)), ((), ())), preferred_element_type=jnp.float32
    )


def local(
    queries, key_codes, key_exps, value_codes, value_exps, d_out, out_weight, prev_psi, mixing
):
    q_local = queries[0]
    grad_out = d_out[0]
    weight = out_weight[0]
    scale = HDIM ** (-0.5)
    kc_all, ke_all, vc_all, ve_all = (
        lax.all_gather(key_codes[0], "seq", axis=0, tiled=True),
        lax.all_gather(key_exps[0], "seq", axis=0, tiled=True),
        lax.all_gather(value_codes[0], "seq", axis=0, tiled=True),
        lax.all_gather(value_exps[0], "seq", axis=0, tiled=True),
    )
    keys = dequant(kc_all, ke_all)
    values = dequant(vc_all, ve_all)
    probs, lses, outputs = ([], [], [])
    for head in range(HEADS):
        cols = slice(head * HDIM, (head + 1) * HDIM)
        scores = inner(q_local[:, cols], keys[:, cols]) * scale
        top = jnp.max(scores, axis=-1, keepdims=True)
        lse = top + jnp.log(jnp.sum(jnp.exp(scores - top), axis=-1, keepdims=True))
        prob = jnp.exp(scores - lse)
        probs.append(prob)
        lses.append(lse)
        outputs.append(
            jnp.dot(
                prob.astype(jnp.bfloat16), values[:, cols], preferred_element_type=jnp.float32
            ).astype(jnp.bfloat16)
        )
    attn = jnp.concatenate(outputs, axis=1)
    weight_b = weight.astype(jnp.bfloat16)
    d_attn = inner(grad_out, lax.all_gather(weight_b, "seq", axis=0, tiled=True)).astype(
        jnp.bfloat16
    )
    grad_w = lax.psum_scatter(
        across(attn, grad_out).astype(jnp.bfloat16), "seq", scatter_dimension=0, tiled=True
    ).astype(jnp.float32)
    dq_list, dots, dk_parts, dv_parts = ([], [], [], [])
    for head in range(HEADS):
        cols = slice(head * HDIM, (head + 1) * HDIM)
        prob = probs[head]
        dprob = inner(d_attn[:, cols], values[:, cols])
        row_dot = jnp.sum(
            d_attn[:, cols].astype(jnp.float32) * attn[:, cols].astype(jnp.float32),
            axis=-1,
            keepdims=True,
        )
        dots.append(row_dot)
        dscore = (prob * (dprob - row_dot) * scale).astype(jnp.bfloat16)
        dq_list.append(
            jnp.dot(dscore, keys[:, cols], preferred_element_type=jnp.float32).astype(jnp.bfloat16)
        )
        dk_parts.append(across(dscore, q_local[:, cols]))
        dv_parts.append(across(prob.astype(jnp.bfloat16), d_attn[:, cols]))
    d_queries = jnp.concatenate(dq_list, axis=1)
    summed_keys, summed_values = (
        lax.psum_scatter(
            jnp.concatenate(dk_parts, axis=1).astype(jnp.bfloat16),
            "seq",
            scatter_dimension=0,
            tiled=True,
        ).astype(jnp.float32),
        lax.psum_scatter(
            jnp.concatenate(dv_parts, axis=1).astype(jnp.bfloat16),
            "seq",
            scatter_dimension=0,
            tiled=True,
        ).astype(jnp.float32),
    )
    d_keys = summed_keys.astype(jnp.bfloat16)
    d_values = summed_values.astype(jnp.bfloat16)
    new_psi = weight - 0.02 * grad_w
    phi = new_psi + weight - prev_psi[0]
    padded = with_halo(phi[None].astype(jnp.bfloat16), (("agent", 0),), 1).astype(jnp.float32)
    numer = mixing[0].astype(jnp.float32)
    before = numer[0]
    after = numer[1]
    own = 16.0 - before - after
    new_weight = (own * phi + before * padded[0] + after * padded[2]) * 0.0625
    return (d_queries[None], d_keys[None], d_values[None], new_weight[None], new_psi[None])


def solution(mesh):
    return jax.shard_map(
        local,
        mesh=mesh,
        in_specs=(
            P("agent", "seq", None),
            P("agent", "seq", None),
            P("agent", "seq", None),
            P("agent", "seq", None),
            P("agent", "seq", None),
            P("agent", "seq", None),
            P("agent", "seq", None),
            P("agent", "seq", None),
            P("agent", None),
        ),
        out_specs=(
            P("agent", "seq", None),
            P("agent", "seq", None),
            P("agent", "seq", None),
            P("agent", "seq", None),
            P("agent", "seq", None),
        ),
        check_vma=False,
    )
```

profile of v0, /device:TPU:1, one launch (start us, length us, event | category | flops | bytes accessed | tf_op | source)
XLA Modules:
  0.0 434.6 jit_solution(7978841883542384914)
XLA Ops:
  8.7 2.1 bitcast_convert_fusion
  10.9 16.0 %all-gather.1 = s32[8,1,8]{2,1,0:T(1,128)S(1)} all-gather(s32[1,1,8]{2,1,0:T(1,128)S(1)} %copy-done.64), channel_id=3, replica_groups=mesh['agent'=16,'seq'=8] {'seq'}, dimensions={0}, use_global_device_ids=true | all-gather | bytes 288 | tf_op jit(solution)/shard_map/all_gather | solution.py:57
  26.9 12.5 %all-gather.3 = s32[8,1,8]{2,1,0:T(1,128)S(1)} all-gather(s32[1,1,8]{2,1,0:T(1,128)S(1)} %copy-done.65), channel_id=5, replica_groups=mesh['agent'=16,'seq'=8] {'seq'}, dimensions={0}, use_global_device_ids=true | all-gather | bytes 288 | tf_op jit(solution)/shard_map/all_gather | solution.py:59
  39.4 25.5 %all-gather.10.cloned.1.call-done = bf16[1,1024,1024]{2,1,0:T(8,128)(2,1)} async-done(((bf16[1,128,1024]{2,1,0:T(8,128)(2,1)}), bf16[1,1024,1024]{2,1,0:T(8,128)(2,1)}) %all-gather.10.cloned.1.call-update) | async-done | bytes 2097168 | tf_op jit(solution)/shard_map/all_gather | solution.py:56
  66.5 2.5 fusion.1
  82.1 35.8 %all-gather.12.cloned.1.call-done = bf16[1,1024,1024]{2,1,0:T(8,128)(2,1)} async-done(((bf16[1,128,1024]{2,1,0:T(8,128)(2,1)}), bf16[1,1024,1024]{2,1,0:T(8,128)(2,1)}) %all-gather.12.cloned.1.call-update) | async-done | bytes 2097168 | tf_op jit(solution)/shard_map/all_gather | solution.py:58
  127.4 82.9 %all-gather.8.cloned.1.call-done = bf16[1024,2048]{1,0:T(8,128)(2,1)} async-done(((bf16[128,2048]{1,0:T(8,128)(2,1)}), bf16[1024,2048]{1,0:T(8,128)(2,1)}) %all-gather.8.cloned.1.call-update) | async-done | bytes 4194320 | tf_op jit(solution)/shard_map/all_gather | solution.py:79
  210.3 3.8 convolution_convert_fusion.17
  215.7 4.2 convolution_convert_fusion
  220.6 2.1 fusion.33
  222.7 2.0 fusion.32
  224.8 2.1 fusion.31
  231.8 4.0 copy.74
  249.5 4.0 copy.72
  256.0 1.9 fusion.49
  257.9 1.8 fusion.48
  261.6 1.9 fusion.46
  263.5 1.9 fusion.45
  265.4 45.9 %reduce-scatter.8.cloned.1.call-done = bf16[128,2048]{1,0:T(8,128)(2,1)} async-done(((bf16[1024,2048]{1,0:T(8,128)(2,1)}), bf16[128,2048]{1,0:T(8,128)(2,1)}) %reduce-scatter.8.cloned.1.call-update) | async-done | bytes 524304 | tf_op jit(solution)/shard_map/reduce_scatter | solution.py:82
  311.3 2.5 fusion.55
  317.6 1.9 fusion.43
  323.2 43.8 %reduce-scatter.12.cloned.1.call-done = bf16[128,1024]{1,0:T(8,128)(2,1)} async-done(((bf16[1024,1024]{1,0:T(8,128)(2,1)}), bf16[128,1024]{1,0:T(8,128)(2,1)}) %reduce-scatter.12.cloned.1.call-update) | async-done | bytes 262160
  369.0 53.0 %reduce-scatter.10.cloned.1.call-done = bf16[128,1024]{1,0:T(8,128)(2,1)} async-done(((bf16[1024,1024]{1,0:T(8,128)(2,1)}), bf16[128,1024]{1,0:T(8,128)(2,1)}) %reduce-scatter.10.cloned.1.call-update) | async-done | bytes 262160
  424.0 3.8 fusion.54
  (219 shorter events, 60.8 us)
Async XLA Ops:
  7.2 203.1 %copy-start = (bf16[1,128,2048]{2,1,0:T(8,128)(2,1)S(1)}, bf16[1,128,2048]{2,1,0:T(8,128)(2,1)}, u32[]{:S(2)}) copy-start(bf16[1,128,2048]{2,1,0:T(8,128)(2,1)} %param.14) | copy-start | bytes 1572868
  7.2 19.7 %copy-start.65 = (s32[1,1,8]{2,1,0:T(1,128)S(1)}, s32[1,1,8]{2,1,0:T(1,128)}, u32[]{:S(2)}) copy-start(s32[1,1,8]{2,1,0:T(1,128)} %param.13) | copy-start | bytes 100
  7.2 57.7 %all-gather.10.cloned.1.call-start = ((), (), s32[]{:S(2)}) async-start(), calls=%async_computation.5 | async-start | bytes 2359296 | tf_op jit(solution)/shard_map/all_gather | solution.py:56
  7.9 110.0 %all-gather.12.cloned.1.call-start = ((), (), s32[]{:S(2)}) async-start(), calls=%async_computation.6 | async-start | bytes 2359296 | tf_op jit(solution)/shard_map/all_gather | solution.py:58
  8.7 201.6 %all-gather.8.cloned.1.call-start = ((), (), s32[]{:S(2)}) async-start(), calls=%async_computation.3 | async-start | bytes 4718592 | tf_op jit(solution)/shard_map/all_gather | solution.py:79
  10.8 300.5 %reduce-scatter.8.cloned.1.call-start = ((), (), s32[]{:S(2)}) async-start(), calls=%async_computation.4 | async-start | bytes 4718592 | tf_op jit(solution)/shard_map/reduce_scatter | solution.py:82
  82.1 40.8 %copy-start.48 = (f32[128]{0:T(128)}, f32[128]{0:T(128)S(1)}, u32[]{:S(2)}) copy-start(f32[128]{0:T(128)S(1)} %log_add_fusion.5) | copy-start | bytes 1540
  82.1 39.8 %copy-start.50 = (f32[128]{0:T(128)}, f32[128]{0:T(128)S(1)}, u32[]{:S(2)}) copy-start(f32[128]{0:T(128)S(1)} %log_add_fusion.6) | copy-start | bytes 1540
  82.1 38.9 %copy-start.52 = (f32[128]{0:T(128)}, f32[128]{0:T(128)S(1)}, u32[]{:S(2)}) copy-start(f32[128]{0:T(128)S(1)} %log_add_fusion.7) | copy-start | bytes 1540
  219.9 147.1 %reduce-scatter.12.cloned.1.call-start = ((), (), s32[]{:S(2)}) async-start(), calls=%async_computation.8 | async-start | bytes 2359296
  220.6 6.3 %copy-start.11 = (f32[1024,128]{1,0:T(8,128)S(1)}, f32[1024,128]{1,0:T(8,128)}, u32[]{:S(2)}) copy-start(f32[1024,128]{1,0:T(8,128)} %copy-done.9) | copy-start | bytes 1572868
  220.6 7.2 %copy-start.7 = (f32[1024,128]{1,0:T(8,128)S(1)}, f32[1024,128]{1,0:T(8,128)}, u32[]{:S(2)}) copy-start(f32[1024,128]{1,0:T(8,128)} %copy-done.5) | copy-start | bytes 1572868
  220.6 8.2 %copy-start.3 = (f32[1024,128]{1,0:T(8,128)S(1)}, f32[1024,128]{1,0:T(8,128)}, u32[]{:S(2)}) copy-start(f32[1024,128]{1,0:T(8,128)} %copy-done.1) | copy-start | bytes 1572868
  235.8 186.2 %reduce-scatter.10.cloned.1.call-start = ((), (), s32[]{:S(2)}) async-start(), calls=%async_computation.7 | async-start | bytes 2359296
  253.5 6.3 %copy-start.39 = (bf16[128,1024]{0,1:T(8,128)(2,1)S(1)}, bf16[128,1024]{0,1:T(8,128)(2,1)}, u32[]{:S(2)}) copy-start(bf16[128,1024]{0,1:T(8,128)(2,1)} %copy-done.38) | copy-start | bytes 786436
  254.1 57.2 %copy-start.20 = (f32[1,128,2048]{2,1,0:T(8,128)S(1)}, f32[1,128,2048]{2,1,0:T(8,128)}, u32[]{:S(2)}) copy-start(f32[1,128,2048]{2,1,0:T(8,128)} %param.15) | copy-start | bytes 3145732
  254.1 57.2 %copy-start.25 = (f32[1,128,2048]{2,1,0:T(8,128)S(1)}, f32[1,128,2048]{2,1,0:T(8,128)}, u32[]{:S(2)}) copy-start(f32[1,128,2048]{2,1,0:T(8,128)} %param.16) | copy-start | bytes 3145732
  256.0 7.5 %copy-start.44 = (bf16[128,1024]{0,1:T(8,128)(2,1)S(1)}, bf16[128,1024]{0,1:T(8,128)(2,1)}, u32[]{:S(2)}) copy-start(bf16[128,1024]{0,1:T(8,128)(2,1)} %copy-done.43) | copy-start | bytes 786436
  265.4 50.4 %copy-start.33 = (bf16[128,1024]{0,1:T(8,128)(2,1)S(1)}, bf16[128,1024]{0,1:T(8,128)(2,1)}, u32[]{:S(2)}) copy-start(bf16[128,1024]{0,1:T(8,128)(2,1)} %copy-done.32) | copy-start | bytes 786436
  265.4 52.3 %copy-start.37 = (bf16[128,1024]{0,1:T(8,128)(2,1)S(1)}, bf16[128,1024]{0,1:T(8,128)(2,1)}, u32[]{:S(2)}) copy-start(bf16[128,1024]{0,1:T(8,128)(2,1)} %copy-done.36) | copy-start | bytes 786436
  311.3 8.2 %copy-start.41 = (bf16[128,1024]{0,1:T(8,128)(2,1)S(1)}, bf16[128,1024]{0,1:T(8,128)(2,1)}, u32[]{:S(2)}) copy-start(bf16[128,1024]{0,1:T(8,128)(2,1)} %copy-done.40) | copy-start | bytes 786436
  313.8 110.2 %collective-permute-start.1 = (bf16[1,128,2048]{2,1,0:T(8,128)(2,1)}, bf16[1,128,2048]{2,1,0:T(8,128)(2,1)}, u32[]{:S(2)}, u32[]{:S(2)}) collective-permute-start(bf16[1,128,2048]{2,1,0:T(8,128)(2,1)} %get-tuple-element.24), channel_id=1, source_target_pairs={{8,0},{16,8},{24,16},{32,24},{40,32},{48,40},{56,48},{64,56},{72,6... | collective-permute-start | bytes 1572872 | tf_op jit(solution)/shard_map/ppermute | solution.py:20
  314.6 109.3 %collective-permute-start = (bf16[1,128,2048]{2,1,0:T(8,128)(2,1)}, bf16[1,128,2048]{2,1,0:T(8,128)(2,1)}, u32[]{:S(2)}, u32[]{:S(2)}) collective-permute-start(bf16[1,128,2048]{2,1,0:T(8,128)(2,1)} %get-tuple-element.24), channel_id=1, source_target_pairs={{0,8},{8,16},{16,24},{24,32},{32,40},{40,48},{48,56},{56,64},{64,7... | collective-permute-start | bytes 1572872 | tf_op jit(solution)/shard_map/ppermute | solution.py:18
  317.6 106.3 %copy-start.28 = (bf16[128,2048]{1,0:T(8,128)(2,1)S(1)}, bf16[128,2048]{1,0:T(8,128)(2,1)}, u32[]{:S(2)}) copy-start(bf16[128,2048]{1,0:T(8,128)(2,1)} %reduce-scatter.8.cloned.1.call-done) | copy-start | bytes 1572868
  (51 other events, 169.5 us)
Sparse Core Ops, SparseCore 0:
  9.7 55.1 all-gather.9
  66.6 51.3 all-gather.11
  120.2 90.0 all-gather.7
  220.1 91.1 reduce-scatter.7
  313.6 53.4 reduce-scatter.11
  369.3 52.6 reduce-scatter.9
where the time goes:
time: 436 us; the launch traced here: 435 us
  waiting for transfers between devices  288 us (66%)
  matrix products  64.4 us (15%)
  blocking collectives  28.5 us (7%)
  local copies, waits for them, and re-layouts  20.7 us (5%)
  between operations  16 us (4%)
  other arithmetic  14.2 us (3%)
    unnamed x8, waiting for transfers between devices  98.3 us
    all_gather x1, waiting for transfers between devices, local(): lax.all_gather(weight_b, 'seq', axis=0, tiled=True)  82.9 us
    reduce_scatter x1, waiting for transfers between devices, local(): lax.psum_scatter(across(attn, grad_out).astype(jnp.bfloat16), 'seq', scat...  45.9 us
    all_gather x1, waiting for transfers between devices, local(): lax.all_gather(value_codes[0], 'seq', axis=0, tiled=True)  35.8 us
    all_gather x1, waiting for transfers between devices, local(): lax.all_gather(key_codes[0], 'seq', axis=0, tiled=True)  25.5 us
    dot_general x17, matrix products, across(): lax.dot_general(left, right, (((0,), (0,)), ((), ())), preferred_element_...  24 us
    unnamed x141, local copies, waits for them, and re-layouts  18.8 us
    dot_general x17, matrix products, inner(): lax.dot_general(left, right, (((1,), (1,)), ((), ())), preferred_element_...  18.1 us
  transfers between devices with their start and end apart: 8, of which 6 were waited for; matrix products, arithmetic and copies ran while one was open for 19% of the time, Pallas kernels for 0%

commit v1 on v0

v1 whole, which is shorter than its diff:
```python
import jax
import jax.numpy as jnp
from jax import lax
from jax.experimental import pallas as pl
from jax.experimental.pallas import tpu as pltpu
from jax.sharding import PartitionSpec as P

HEADS = 8
HDIM = 128
TOK = 128
N_SEQ = 8
N_AGENT = 16
TOKENS = N_SEQ * TOK
HD = HEADS * HDIM
D = 2048
PAIR = 2 * TOK
N_PAIR = TOKENS // PAIR
SCALE = HDIM ** (-0.5)
MESH = pl.DeviceIdType.MESH

A1, A2, B1, B2 = (0, 640), (640, 512), (1152, 384), (1536, 512)
PIECES = {"A1": A1, "A2": A2, "B1": B1, "B2": B2}


def _gather_messages():
    msgs = []
    for p in ("B1", "B2", "A1", "A2"):
        msgs.append(("P" + p, "dn", (-1, 0), p))
        msgs.append(("M" + p, "up", (1, 0), p))
        msgs.append(("X" + p, "xp", (0, 1), p))
    for p in ("A1", "A2"):
        msgs.append(("PX" + p, "dn", (-1, 1), p))
        msgs.append(("MX" + p, "up", (1, 1), p))
    msgs.append(("P2A1", "dn", (-2, 0), "A1"))
    msgs.append(("P2XA1", "dn", (-2, 1), "A1"))
    msgs.append(("P2B1", "dn", (-2, 0), "B1"))
    msgs.append(("M2A2", "up", (2, 0), "A2"))
    msgs.append(("M2XA2", "up", (2, 1), "A2"))
    msgs.append(("M2B2", "up", (2, 0), "B2"))
    for p in ("B1", "B2"):
        msgs.append(("XP" + p, "xp", (-1, 1), p))
        msgs.append(("XM" + p, "xp", (1, 1), p))
    msgs.append(("XP2B1", "xp", (-2, 1), "B1"))
    msgs.append(("XM2B2", "xp", (2, 1), "B2"))
    return msgs


MSGS = _gather_messages()
KIND = {m[0]: i for i, m in enumerate(MSGS)}
N_MSG = len(MSGS)


def nt(a, b):
    return lax.dot_general(a, b, (((1,), (1,)), ((), ())), preferred_element_type=jnp.float32)


def nn(a, b):
    return jnp.dot(a, b, preferred_element_type=jnp.float32)


def kernel(
    mix_ref, ke_ref, ve_ref, q_hbm, kc_hbm, vc_hbm, do_hbm, w_hbm, ps_hbm,
    dq_out, dk_out, dv_out, nw_out, np_out,
    kc_v, vc_v, k_st, v_st, qh, kh, vh, kt, vt, do_all, w_f, ps_f, w_t,
    pt, at, gw, dk_acc, dv_acc, dq_st, dk_st, dv_st, phi_b, halo,
    load_sem, own_sem, a2a_s, a2a_r, ag_s, ag_r, back_s, back_r, halo_s, halo_r,
):
    me = lax.axis_index("seq")
    agent = lax.axis_index("agent")
    y, x = me // 2, lax.rem(me, 2)

    def at_rel(dy, dx):
        return lax.rem(y + (dy + 8), 4) * 2 + lax.rem(x + dx, 2)

    def rows(block):
        return pl.ds(pl.multiple_of(block * TOK, TOK), TOK)

    def cols(block):
        return pl.ds(pl.multiple_of(block * HDIM, HDIM), HDIM)

    rels = [(dy, dx) for dy in range(4) for dx in range(2)]
    peers = rels[1:]

    loads = {}
    for i, (name, src, dst) in enumerate(
        (
            ("k", kc_hbm, kc_v),
            ("v", vc_hbm, vc_v),
            ("q", q_hbm.at[:, cols(me)], qh.at[rows(me), :]),
            ("w", w_hbm, w_f),
            ("d", do_hbm, do_all.at[rows(me), :]),
            ("p", ps_hbm, ps_f),
        )
    ):
        loads[name] = pltpu.make_async_copy(src, dst, load_sem.at[i])
        loads[name].start()

    barrier = pltpu.get_barrier_semaphore()
    for dy, dx in peers:
        pl.semaphore_signal(barrier, inc=1, device_id={"seq": at_rel(dy, dx)}, device_id_type=MESH)
    nxt, prv = lax.rem(agent + 1, N_AGENT), lax.rem(agent + N_AGENT - 1, N_AGENT)
    for other in (nxt, prv):
        pl.semaphore_signal(barrier, inc=1, device_id={"agent": other}, device_id_type=MESH)
    pl.semaphore_wait(barrier, len(peers) + 2)

    sent = []

    def push(src, dst, ssem, rsem, target):
        copy = pltpu.make_async_remote_copy(
            src_ref=src, dst_ref=dst, send_sem=ssem, recv_sem=rsem,
            device_id=target, device_id_type=MESH,
        )
        copy.start()
        sent.append(copy)

    def arrived(dst, rsem, ssem):
        pltpu.make_async_remote_copy(
            src_ref=dst, dst_ref=dst, send_sem=ssem, recv_sem=rsem,
            device_id={"seq": at_rel(0, 1)}, device_id_type=MESH,
        ).wait_recv()

    def a2a_send(j, src, dst):
        for r, (dy, dx) in enumerate(rels):
            if r:
                t = at_rel(dy, dx)
                push(src.at[:, cols(t)], dst.at[rows(me), :], a2a_s.at[j, r], a2a_r.at[j, r],
                     {"seq": t})

    def a2a_wait(j, dst):
        for r, (dy, dx) in enumerate(rels):
            if r:
                arrived(dst.at[rows(at_rel(-dy, dx)), :], a2a_r.at[j, r], a2a_s.at[j, r])

    def scaled(codes, expo, out):
        factor = jnp.exp2(expo[...].astype(jnp.float32))
        for h in range(HEADS):
            c = slice(h * HDIM, (h + 1) * HDIM)
            out[:, c] = (codes[:, c].astype(jnp.float32) * factor[0:1, h : h + 1]).astype(
                jnp.bfloat16
            )

    a2a_send(0, q_hbm, qh)
    loads["k"].wait()
    scaled(kc_v, ke_ref, k_st)
    a2a_send(1, k_st, kh)
    loads["v"].wait()
    scaled(vc_v, ve_ref, v_st)
    a2a_send(2, v_st, vh)

    step = {"xp": (0, 1), "up": (1, 0), "dn": (-1, 0)}
    back_to = {"xp": "xp", "up": "dn", "dn": "up"}

    def ag_send(name, own=False):
        kind = KIND[name]
        _, source, (dy, dx), piece = MSGS[kind]
        sy, sx = step[source]
        ty, tx = step[back_to[source]]
        block = at_rel(dy - sy, (dx + sx) % 2)
        first, width = PIECES[piece]
        here = do_all.at[rows(block), pl.ds(first, width)]
        src = do_hbm.at[:, pl.ds(first, width)] if own else here
        push(src, here, ag_s.at[kind], ag_r.at[kind], {"seq": at_rel(ty, tx)})

    def ag_wait(name):
        kind = KIND[name]
        _, _, (dy, dx), piece = MSGS[kind]
        first, width = PIECES[piece]
        arrived(do_all.at[rows(at_rel(dy, dx)), pl.ds(first, width)], ag_r.at[kind], ag_s.at[kind])

    for name in ("PB1", "MB2", "XA1", "PB2", "MB1", "XA2", "PA1", "MA2", "PA2", "MA1", "XB1", "XB2"):
        ag_send(name, own=True)

    own_k = pltpu.make_async_copy(k_st.at[:, cols(me)], kh.at[rows(me), :], own_sem.at[0])
    own_v = pltpu.make_async_copy(v_st.at[:, cols(me)], vh.at[rows(me), :], own_sem.at[1])
    own_k.start()
    own_v.start()

    loads["w"].wait()
    for c in range(0, D, 256):
        w_t[c : c + 256, :] = w_f[:, c : c + 256].T.astype(jnp.bfloat16)
    dk_acc[...] = jnp.zeros_like(dk_acc)
    dv_acc[...] = jnp.zeros_like(dv_acc)
    gw[...] = jnp.zeros_like(gw)

    def stage_b():
        ag_wait("PB1")
        ag_send("P2B1")
        ag_send("XPB1")
        ag_wait("MB2")
        ag_send("M2B2")
        ag_send("XMB2")
        ag_wait("PB2")
        ag_send("XPB2")
        ag_wait("MB1")
        ag_send("XMB1")

    def stage_x():
        ag_wait("XA1")
        ag_send("PXA1")
        ag_send("MXA1")
        ag_wait("XA2")
        ag_send("PXA2")
        ag_send("MXA2")

    def stage_a():
        ag_wait("PA1")
        ag_send("P2A1")
        ag_wait("MA2")
        ag_send("M2A2")

    def stage_2b():
        ag_wait("P2B1")
        ag_send("XP2B1")
        ag_wait("M2B2")
        ag_send("XM2B2")

    def stage_xa():
        ag_wait("PXA1")
        ag_send("P2XA1")
        ag_wait("MXA2")
        ag_send("M2XA2")

    def forward(p):
        q = qh[p * PAIR : (p + 1) * PAIR, :]
        s = nt(kh[...], q) * SCALE
        e = jnp.exp(s - jnp.max(s, axis=0, keepdims=True))
        prob = e / jnp.sum(e, axis=0, keepdims=True)
        pt[p] = prob
        at[p] = nn(vt[...], prob.astype(jnp.bfloat16)).astype(jnp.bfloat16)

    def pair_of(dy):
        return lax.rem(y + (dy + 8), 4)

    def prows(pair):
        return pl.ds(pl.multiple_of(pair * PAIR, PAIR), PAIR)

    def add_grad(dy):
        pair = pair_of(dy)
        gw[...] += nn(at[pair], do_all[prows(pair), :])

    def backward(dy):
        pair = pair_of(dy)
        q = qh[prows(pair), :]
        d_f = nn(do_all[prows(pair), :], w_t[...])
        d_b = d_f.astype(jnp.bfloat16)
        d_t = d_b.astype(jnp.float32).T
        row_dot = jnp.sum(d_t * at[pair].astype(jnp.float32), axis=0, keepdims=True)
        prob = pt[pair]
        d_s = (prob * (nt(vh[...], d_b) - row_dot) * SCALE).astype(jnp.bfloat16)
        dk_acc[...] += nn(d_s, q)
        dv_acc[...] += nn(prob.astype(jnp.bfloat16), d_b)
        dq_st[prows(pair), :] = nn(kt[...], d_s).T.astype(jnp.bfloat16)

    def send_rows(j, st, out, dy):
        for dx in range(2):
            r = (dy % 4) * 2 + dx
            t = at_rel(dy, dx)
            if r:
                push(st.at[rows(t), :], out.at[:, cols(me)], back_s.at[j, r], back_r.at[j, r],
                     {"seq": t})

    outs = ((dq_st, dq_out), (dk_st, dk_out), (dv_st, dv_out))

    stage_b()
    stage_x()
    own_k.wait()
    own_v.wait()
    loads["q"].wait()
    a2a_wait(0, qh)
    a2a_wait(1, kh)
    a2a_wait(2, vh)
    kt[...] = kh[...].astype(jnp.float32).T.astype(jnp.bfloat16)
    vt[...] = vh[...].astype(jnp.float32).T.astype(jnp.bfloat16)
    forward(0)
    stage_a()
    forward(1)
    stage_2b()
    forward(2)
    stage_xa()
    forward(3)

    loads["d"].wait()
    ag_wait("XB1")
    ag_wait("XB2")
    add_grad(0)
    backward(0)
    send_rows(0, dq_st, dq_out, 0)

    for name in ("PA2", "PXA2", "XPB1", "XPB2"):
        ag_wait(name)
    add_grad(-1)
    backward(-1)
    send_rows(0, dq_st, dq_out, -1)

    for name in ("MA1", "MXA1", "XMB1", "XMB2"):
        ag_wait(name)
    add_grad(1)
    backward(1)
    send_rows(0, dq_st, dq_out, 1)

    for name in ("P2A1", "M2A2", "P2XA1", "M2XA2", "XP2B1", "XM2B2"):
        ag_wait(name)
    add_grad(2)

    loads["p"].wait()
    new_psi = w_f[...] - 0.02 * gw[...]
    np_out[...] = new_psi
    phi = new_psi + w_f[...] - ps_f[...]
    gw[...] = phi
    phi_b[...] = phi.astype(jnp.bfloat16)
    for i, other in enumerate((nxt, prv)):
        push(phi_b, halo.at[i], halo_s.at[i], halo_r.at[i], {"agent": other})

    backward(2)
    dk_st[...] = dk_acc[...].astype(jnp.bfloat16)
    dv_st[...] = dv_acc[...].astype(jnp.bfloat16)
    for dy in (2, 1, -1, 0):
        send_rows(1, dk_st, dk_out, dy)
        send_rows(2, dv_st, dv_out, dy)
    send_rows(0, dq_st, dq_out, 2)
    own = []
    for j, (st, out) in enumerate(outs):
        own.append(pltpu.make_async_copy(st.at[rows(me), :], out.at[:, cols(me)], own_sem.at[2 + j]))
        own[-1].start()

    for i in range(2):
        arrived(halo.at[i], halo_r.at[i], halo_s.at[i])
    before = mix_ref[0, 0].astype(jnp.float32)
    after = mix_ref[0, 1].astype(jnp.float32)
    nw_out[...] = (
        (16.0 - before - after) * gw[...]
        + before * halo[0].astype(jnp.float32)
        + after * halo[1].astype(jnp.float32)
    ) * 0.0625

    for j, (st, out) in enumerate(outs):
        own[j].wait()
        for r, (dy, dx) in enumerate(rels):
            if r:
                arrived(out.at[:, cols(at_rel(-dy, dx))], back_r.at[j, r], back_s.at[j, r])
    for copy in sent:
        copy.wait_send()


def local(
    queries, key_codes, key_exps, value_codes, value_exps, d_out, out_weight, prev_psi, mixing
):
    bf, f32 = jnp.bfloat16, jnp.float32
    vmem = pl.BlockSpec(memory_space=pltpu.VMEM)
    smem = pl.BlockSpec(memory_space=pltpu.SMEM)
    hbm = pl.BlockSpec(memory_space=pl.ANY)
    outs = pl.pallas_call(
        kernel,
        out_shape=[
            jax.ShapeDtypeStruct((TOK, HD), bf),
            jax.ShapeDtypeStruct((TOK, HD), bf),
            jax.ShapeDtypeStruct((TOK, HD), bf),
            jax.ShapeDtypeStruct((HDIM, D), f32),
            jax.ShapeDtypeStruct((HDIM, D), f32),
        ],
        in_specs=[smem, vmem, vmem] + [hbm] * 6,
        out_specs=[vmem] * 5,
        scratch_shapes=[
            pltpu.VMEM((TOK, HD), bf),
            pltpu.VMEM((TOK, HD), bf),
            pltpu.VMEM((TOK, HD), bf),
            pltpu.VMEM((TOK, HD), bf),
            pltpu.VMEM((TOKENS, HDIM), bf),
            pltpu.VMEM((TOKENS, HDIM), bf),
            pltpu.VMEM((TOKENS, HDIM), bf),
            pltpu.VMEM((HDIM, TOKENS), bf),
            pltpu.VMEM((HDIM, TOKENS), bf),
            pltpu.VMEM((TOKENS, D), bf),
            pltpu.VMEM((HDIM, D), f32),
            pltpu.VMEM((HDIM, D), f32),
            pltpu.VMEM((D, HDIM), bf),
            pltpu.VMEM((N_PAIR, TOKENS, PAIR), f32),
            pltpu.VMEM((N_PAIR, HDIM, PAIR), bf),
            pltpu.VMEM((HDIM, D), f32),
            pltpu.VMEM((TOKENS, HDIM), f32),
            pltpu.VMEM((TOKENS, HDIM), f32),
            pltpu.VMEM((TOKENS, HDIM), bf),
            pltpu.VMEM((TOKENS, HDIM), bf),
            pltpu.VMEM((TOKENS, HDIM), bf),
            pltpu.VMEM((HDIM, D), bf),
            pltpu.VMEM((2, HDIM, D), bf),
            pltpu.SemaphoreType.DMA((6,)),
            pltpu.SemaphoreType.DMA((5,)),
            pltpu.SemaphoreType.DMA((3, N_SEQ)),
            pltpu.SemaphoreType.DMA((3, N_SEQ)),
            pltpu.SemaphoreType.DMA((N_MSG,)),
            pltpu.SemaphoreType.DMA((N_MSG,)),
            pltpu.SemaphoreType.DMA((3, N_SEQ)),
            pltpu.SemaphoreType.DMA((3, N_SEQ)),
            pltpu.SemaphoreType.DMA((2,)),
            pltpu.SemaphoreType.DMA((2,)),
        ],
        compiler_params=pltpu.CompilerParams(
            collective_id=0, has_side_effects=True, vmem_limit_bytes=50 * 1024 * 1024
        ),
        cost_estimate=pl.CostEstimate(
            flops=2 * TOKENS * HDIM * (2 * D + 6 * TOKENS),
            bytes_accessed=8 * 1024 * 1024,
            transcendentals=TOKENS * TOKENS,
        ),
        name="exact_diffusion_step",
    )(
        mixing, key_exps[0], value_exps[0], queries[0], key_codes[0], value_codes[0],
        d_out[0], out_weight[0], prev_psi[0],
    )
    return tuple(out[None] for out in outs)


def solution(mesh):
    rows = P("agent", "seq", None)
    return jax.shard_map(
        local,
        mesh=mesh,
        in_specs=(rows,) * 8 + (P("agent", None),),
        out_specs=(rows,) * 5,
        check_vma=False,
    )
```

time: 436 us -> 70.8 us (0.16)
  the two profiles are of different devices: /device:TPU:1 before, /device:TPU:0 now
where the time goes in v1:
time: 70.8 us; the launch traced here: 70.5 us
  Pallas kernels  60.6 us (86%)
  local copies, waits for them, and re-layouts  9.23 us (13%)
    pallas_call x1, Pallas kernels, local(): pl.pallas_call(kernel, out_shape=[jax.ShapeDtypeStruct((TOK, HD), bf), ja...  60.6 us
    unnamed x21, local copies, waits for them, and re-layouts  9.23 us

profile of v1, /device:TPU:0, one launch (start us, length us, event | category | flops | bytes accessed | tf_op | source)
XLA Modules:
  0.0 70.5 jit_solution(1445792552376179548)
XLA Ops:
  0.6 0.0 copy-start.4
  0.6 0.0 copy-start.5
  0.7 0.0 copy-start.6
  0.7 0.6 copy-done.4
  1.3 0.0 copy-done.5
  1.3 0.0 copy-done.6
  1.3 0.0 copy-start
  1.3 1.0 %copy-done = bf16[1,128,2048]{2,1,0:T(8,128)(2,1)S(1)} copy-done((bf16[1,128,2048]{2,1,0:T(8,128)(2,1)S(1)}, bf16[1,128,2048]{2,1,0:T(8,128)(2,1)}, u32[]{:S(2)}) %copy-start) | copy-done | bytes 524312
  2.4 0.0 copy-start.1
  2.4 0.9 %copy-done.1 = bf16[1,128,1024]{2,1,0:T(8,128)(2,1)S(1)} copy-done((bf16[1,128,1024]{2,1,0:T(8,128)(2,1)S(1)}, bf16[1,128,1024]{2,1,0:T(8,128)(2,1)}, u32[]{:S(2)}) %copy-start.1) | copy-done | bytes 262168
  3.3 0.0 copy-start.2
  3.3 0.9 %copy-done.2 = bf16[1,128,1024]{2,1,0:T(8,128)(2,1)S(1)} copy-done((bf16[1,128,1024]{2,1,0:T(8,128)(2,1)S(1)}, bf16[1,128,1024]{2,1,0:T(8,128)(2,1)}, u32[]{:S(2)}) %copy-start.2) | copy-done | bytes 262168
  4.3 0.0 copy-start.3
  4.3 0.9 %copy-done.3 = bf16[1,128,1024]{2,1,0:T(8,128)(2,1)S(1)} copy-done((bf16[1,128,1024]{2,1,0:T(8,128)(2,1)S(1)}, bf16[1,128,1024]{2,1,0:T(8,128)(2,1)}, u32[]{:S(2)}) %copy-start.3) | copy-done | bytes 262168
  5.2 60.6 %exact_diffusion_step.1 = (bf16[128,1024]{1,0:T(8,128)(2,1)S(1)}, bf16[128,1024]{1,0:T(8,128)(2,1)S(1)}, bf16[128,1024]{1,0:T(8,128)(2,1)S(1)}, f32[128,2048]{1,0:T(8,128)S(1)}, f32[128,2048]{1,0:T(8,128)}) custom-call(s32[1,2]{1,0:T(1,128)S(1)} %copy-done.4, s32[1,8]{1,0:T(1,128)S(1)} %bitcast.21, s32[1,8]{1,0:T(1,128)S(1)} %bitcast.22, ...), custom_call_target="tpu_custom_call" | custom-call | flops 2684354560 | bytes 8388608 | tf_op jit(solution)/shard_map/exact_diffusion_step/pallas_call | solution.py:352
  65.8 0.7 %copy.19 = bf16[1,128,1024]{2,1,0:T(8,128)(2,1)} copy(bf16[1,128,1024]{2,1,0:T(8,128)(2,1)S(1)} %bitcast.16) | data formatting | bytes 524288
  66.5 0.7 copy.20
  67.2 0.7 copy.21
  67.9 0.0 copy-start.7
  67.9 1.0 %copy.22 = f32[1,128,2048]{2,1,0:T(8,128)} copy(f32[1,128,2048]{2,1,0:T(8,128)S(1)} %bitcast.13) | data formatting | bytes 2097152
  68.9 0.6 copy-done.7
  69.5 1.0 %copy.23 = f32[1,128,2048]{2,1,0:T(8,128)} copy(f32[1,128,2048]{2,1,0:T(8,128)S(1)} %bitcast.23) | data formatting | bytes 2097152
Async XLA Ops:
  0.6 0.7 copy-start.4
  0.6 0.7 copy-start.5
  0.7 0.7 copy-start.6
  1.3 1.0 %copy-start = (bf16[1,128,2048]{2,1,0:T(8,128)(2,1)S(1)}, bf16[1,128,2048]{2,1,0:T(8,128)(2,1)}, u32[]{:S(2)}) copy-start(bf16[1,128,2048]{2,1,0:T(8,128)(2,1)} %param.14) | copy-start | bytes 1572868
  2.4 0.9 %copy-start.1 = (bf16[1,128,1024]{2,1,0:T(8,128)(2,1)S(1)}, bf16[1,128,1024]{2,1,0:T(8,128)(2,1)}, u32[]{:S(2)}) copy-start(bf16[1,128,1024]{2,1,0:T(8,128)(2,1)} %param.9) | copy-start | bytes 786436
  3.3 0.9 %copy-start.2 = (bf16[1,128,1024]{2,1,0:T(8,128)(2,1)S(1)}, bf16[1,128,1024]{2,1,0:T(8,128)(2,1)}, u32[]{:S(2)}) copy-start(bf16[1,128,1024]{2,1,0:T(8,128)(2,1)} %param.10) | copy-start | bytes 786436
  4.3 0.9 %copy-start.3 = (bf16[1,128,1024]{2,1,0:T(8,128)(2,1)S(1)}, bf16[1,128,1024]{2,1,0:T(8,128)(2,1)}, u32[]{:S(2)}) copy-start(bf16[1,128,1024]{2,1,0:T(8,128)(2,1)} %param.12) | copy-start | bytes 786436
  67.9 1.6 %copy-start.7 = (f32[128,2048]{1,0:T(8,128)S(1)}, f32[128,2048]{1,0:T(8,128)}, u32[]{:S(2)}) copy-start(f32[128,2048]{1,0:T(8,128)} %get-tuple-element.14) | copy-start | bytes 3145732

commit v2 on v1

--- a/solution.py
+++ b/solution.py
@@ -15,6 +15,7 @@
 D = 2048
 PAIR = 2 * TOK
 N_PAIR = TOKENS // PAIR
+VMEM = 62 * 1024 * 1024
 SCALE = HDIM ** (-0.5)
 MESH = pl.DeviceIdType.MESH
 
@@ -59,11 +60,11 @@
 
 
 def kernel(
-    mix_ref, ke_ref, ve_ref, q_hbm, kc_hbm, vc_hbm, do_hbm, w_hbm, ps_hbm,
-    dq_out, dk_out, dv_out, nw_out, np_out,
-    kc_v, vc_v, k_st, v_st, qh, kh, vh, kt, vt, do_all, w_f, ps_f, w_t,
-    pt, at, gw, dk_acc, dv_acc, dq_st, dk_st, dv_st, phi_b, halo,
-    load_sem, own_sem, a2a_s, a2a_r, ag_s, ag_r, back_s, back_r, halo_s, halo_r,
+    ke_hbm, ve_hbm, q_hbm, kc_hbm, vc_hbm, do_hbm, w_hbm, ps_hbm,
+    dq_out, dk_out, dv_out, np_out, phi_out, halo_out,
+    ke_ref, ve_ref, kc_v, vc_v, k_st, v_st, qh, kh, vh, kt, vt, do_all, w_f, ps_f, w_t,
+    pt, at, gw, dk_acc, dv_acc, dq_st, dk_st, dv_st, phi_f, phi_b,
+    load_sem, own_sem, out_sem, a2a_s, a2a_r, ag_s, ag_r, back_s, back_r, halo_s, halo_r,
 ):
     me = lax.axis_index("seq")
     agent = lax.axis_index("agent")
@@ -84,7 +85,9 @@
     loads = {}
     for i, (name, src, dst) in enumerate(
         (
+            ("ke", ke_hbm, ke_ref),
             ("k", kc_hbm, kc_v),
+            ("ve", ve_hbm, ve_ref),
             ("v", vc_hbm, vc_v),
             ("q", q_hbm.at[:, cols(me)], qh.at[rows(me), :]),
             ("w", w_hbm, w_f),
@@ -140,9 +143,11 @@
             )
 
     a2a_send(0, q_hbm, qh)
+    loads["ke"].wait()
     loads["k"].wait()
     scaled(kc_v, ke_ref, k_st)
     a2a_send(1, k_st, kh)
+    loads["ve"].wait()
     loads["v"].wait()
     scaled(vc_v, ve_ref, v_st)
     a2a_send(2, v_st, vh)
@@ -304,12 +309,18 @@
 
     loads["p"].wait()
     new_psi = w_f[...] - 0.02 * gw[...]
-    np_out[...] = new_psi
     phi = new_psi + w_f[...] - ps_f[...]
-    gw[...] = phi
     phi_b[...] = phi.astype(jnp.bfloat16)
     for i, other in enumerate((nxt, prv)):
-        push(phi_b, halo.at[i], halo_s.at[i], halo_r.at[i], {"agent": other})
+        push(phi_b, halo_out.at[i], halo_s.at[i], halo_r.at[i], {"agent": other})
+    gw[...] = new_psi
+    phi_f[...] = phi
+    stores = [
+        pltpu.make_async_copy(gw, np_out, out_sem.at[0]),
+        pltpu.make_async_copy(phi_f, phi_out, out_sem.at[1]),
+    ]
+    for copy in stores:
+        copy.start()
 
     backward(2)
     dk_st[...] = dk_acc[...].astype(jnp.bfloat16)
@@ -324,15 +335,9 @@
         own[-1].start()
 
     for i in range(2):
-        arrived(halo.at[i], halo_r.at[i], halo_s.at[i])
-    before = mix_ref[0, 0].astype(jnp.float32)
-    after = mix_ref[0, 1].astype(jnp.float32)
-    nw_out[...] = (
-        (16.0 - before - after) * gw[...]
-        + before * halo[0].astype(jnp.float32)
-        + after * halo[1].astype(jnp.float32)
-    ) * 0.0625
-
+        arrived(halo_out.at[i], halo_r.at[i], halo_s.at[i])
+    for copy in stores:
+        copy.wait()
     for j, (st, out) in enumerate(outs):
         own[j].wait()
         for r, (dy, dx) in enumerate(rels):
@@ -342,25 +347,51 @@
         copy.wait_send()
 
 
+def finish(
+    mix_hbm, dq, dk, dv, psi, phi, halo, dq_out, dk_out, dv_out, nw_out, np_out,
+    mix, phi_v, halo_v, load_sem, sem,
+):
+    loads = [
+        pltpu.make_async_copy(a, b, load_sem.at[i])
+        for i, (a, b) in enumerate(((mix_hbm, mix), (phi, phi_v), (halo, halo_v)))
+    ]
+    for copy in loads:
+        copy.start()
+    copies = [
+        pltpu.make_async_copy(a, b, sem.at[i])
+        for i, (a, b) in enumerate(((psi, np_out), (dq, dq_out), (dk, dk_out), (dv, dv_out)))
+    ]
+    for copy in copies:
+        copy.start()
+    for copy in loads:
+        copy.wait()
+    before = mix[0, 0].astype(jnp.float32)
+    after = mix[0, 1].astype(jnp.float32)
+    phi_v[...] = (
+        (16.0 - before - after) * phi_v[...]
+        + before * halo_v[0].astype(jnp.float32)
+        + after * halo_v[1].astype(jnp.float32)
+    ) * 0.0625
+    copies.append(pltpu.make_async_copy(phi_v, nw_out, sem.at[4]))
+    copies[-1].start()
+    for copy in copies:
+        copy.wait()
+
+
 def local(
     queries, key_codes, key_exps, value_codes, value_exps, d_out, out_weight, prev_psi, mixing
 ):
     bf, f32 = jnp.bfloat16, jnp.float32
-    vmem = pl.BlockSpec(memory_space=pltpu.VMEM)
-    smem = pl.BlockSpec(memory_space=pltpu.SMEM)
-    hbm = pl.BlockSpec(memory_space=pl.ANY)
-    outs = pl.pallas_call(
+    hbm = pl.BlockSpec(memory_space=pltpu.HBM)
+    small, large = jax.ShapeDtypeStruct((TOK, HD), bf), jax.ShapeDtypeStruct((HDIM, D), f32)
+    *grads, psi, phi, halo = pl.pallas_call(
         kernel,
-        out_shape=[
-            jax.ShapeDtypeStruct((TOK, HD), bf),
-            jax.ShapeDtypeStruct((TOK, HD), bf),
-            jax.ShapeDtypeStruct((TOK, HD), bf),
-            jax.ShapeDtypeStruct((HDIM, D), f32),
-            jax.ShapeDtypeStruct((HDIM, D), f32),
-        ],
-        in_specs=[smem, vmem, vmem] + [hbm] * 6,
-        out_specs=[vmem] * 5,
+        out_shape=[small] * 3 + [large] * 2 + [jax.ShapeDtypeStruct((2, HDIM, D), bf)],
+        in_specs=[hbm] * 8,
+        out_specs=[hbm] * 6,
         scratch_shapes=[
+            pltpu.VMEM((1, HEADS), jnp.int32),
+            pltpu.VMEM((1, HEADS), jnp.int32),
             pltpu.VMEM((TOK, HD), bf),
             pltpu.VMEM((TOK, HD), bf),
             pltpu.VMEM((TOK, HD), bf),
@@ -382,10 +413,11 @@
             pltpu.VMEM((TOKENS, HDIM), bf),
             pltpu.VMEM((TOKENS, HDIM), bf),
             pltpu.VMEM((TOKENS, HDIM), bf),
+            pltpu.VMEM((HDIM, D), f32),
             pltpu.VMEM((HDIM, D), bf),
-            pltpu.VMEM((2, HDIM, D), bf),
-            pltpu.SemaphoreType.DMA((6,)),
+            pltpu.SemaphoreType.DMA((8,)),
             pltpu.SemaphoreType.DMA((5,)),
+            pltpu.SemaphoreType.DMA((2,)),
             pltpu.SemaphoreType.DMA((3, N_SEQ)),
             pltpu.SemaphoreType.DMA((3, N_SEQ)),
             pltpu.SemaphoreType.DMA((N_MSG,)),
@@ -396,7 +428,7 @@
             pltpu.SemaphoreType.DMA((2,)),
         ],
         compiler_params=pltpu.CompilerParams(
-            collective_id=0, has_side_effects=True, vmem_limit_bytes=50 * 1024 * 1024
+            collective_id=0, has_side_effects=True, vmem_limit_bytes=VMEM
         ),
         cost_estimate=pl.CostEstimate(
             flops=2 * TOKENS * HDIM * (2 * D + 6 * TOKENS),
@@ -405,9 +437,24 @@
         ),
         name="exact_diffusion_step",
     )(
-        mixing, key_exps[0], value_exps[0], queries[0], key_codes[0], value_codes[0],
+        key_exps[0], value_exps[0], queries[0], key_codes[0], value_codes[0],
         d_out[0], out_weight[0], prev_psi[0],
     )
+    outs = pl.pallas_call(
+        finish,
+        out_shape=[small] * 3 + [large] * 2,
+        in_specs=[hbm] * 7,
+        out_specs=[hbm] * 5,
+        scratch_shapes=[
+            pltpu.SMEM((1, 2), jnp.int32),
+            pltpu.VMEM((HDIM, D), f32),
+            pltpu.VMEM((2, HDIM, D), bf),
+            pltpu.SemaphoreType.DMA((3,)),
+            pltpu.SemaphoreType.DMA((5,)),
+        ],
+        compiler_params=pltpu.CompilerParams(vmem_limit_bytes=VMEM),
+        name="finish",
+    )(mixing, *grads, psi, phi, halo)
     return tuple(out[None] for out in outs)
 
 

time: 70.8 us -> 117 us (1.65)
  Pallas kernels: 60.6 us -> 116 us
  local copies, waits for them, and re-layouts: 9.23 us -> 0 us
    pallas_call x1 -> x2, Pallas kernels: 60.6 us -> 116 us  [the longest x1 59.2 us: local(): pl.pallas_call(kernel, out_shape=[small] * 3 + [large] * 2 + [jax.ShapeDt...]
    unnamed x21 -> x0, local copies, waits for them, and re-layouts: 9.23 us -> none
where the time goes in v2:
time: 117 us
  Pallas kernels  116 us (99%)
    pallas_call x1, Pallas kernels, local(): pl.pallas_call(kernel, out_shape=[small] * 3 + [large] * 2 + [jax.ShapeDt...  59.2 us
    pallas_call x1, Pallas kernels, local(): pl.pallas_call(finish, out_shape=[small] * 3 + [large] * 2, in_specs=[hbm...  56.8 us

profile of v2, /device:TPU:0, one launch (start us, length us, event | category | flops | bytes accessed | tf_op | source)
XLA Modules:
  0.0 116.6 jit_solution(6874038434929491039)
XLA Ops:
  0.6 59.2 %exact_diffusion_step.1 = (bf16[128,1024]{1,0:T(8,128)(2,1)}, bf16[128,1024]{1,0:T(8,128)(2,1)}, bf16[128,1024]{1,0:T(8,128)(2,1)}, f32[128,2048]{1,0:T(8,128)},...) custom-call(s32[1,8]{1,0:T(1,128)} %bitcast.24, s32[1,8]{1,0:T(1,128)} %bitcast.25, bf16[128,1024]{1,0:T(8,128)(2,1)} %bitcast.18, ...), custom_call_target="tpu_custom_call" | custom-call | flops 2684354560 | bytes 8388608 | tf_op jit(solution)/shard_map/exact_diffusion_step/pallas_call | solution.py:387
  59.8 56.8 %finish.1 = (bf16[128,1024]{1,0:T(8,128)(2,1)}, bf16[128,1024]{1,0:T(8,128)(2,1)}, bf16[128,1024]{1,0:T(8,128)(2,1)}, f32[128,2048]{1,0:T(8,128)}, f32[128,2048]{1,0:T(8,128)}) custom-call(s32[1,2]{1,0:T(1,128)} %mix_hbm.1, bf16[128,1024]{1,0:T(8,128)(2,1)} %get-tuple-element.16.dq, bf16[128,1024]{1,0:T(8,128)(2,1)} %get-tuple-element.17.dk, ...), custom_call_target="tpu_custom_call" | custom-call | tf_op jit(solution)/shard_map/finish/pallas_call | solution.py:443

commit v3 on v2

--- a/solution.py
+++ b/solution.py
@@ -16,10 +16,12 @@
 PAIR = 2 * TOK
 N_PAIR = TOKENS // PAIR
 VMEM = 62 * 1024 * 1024
+CHUNK = 32
+N_CHUNK = HDIM // CHUNK
 SCALE = HDIM ** (-0.5)
 MESH = pl.DeviceIdType.MESH
 
-A1, A2, B1, B2 = (0, 640), (640, 512), (1152, 384), (1536, 512)
+A1, A2, B1, B2 = (0, 640), (640, 640), (1280, 384), (1664, 384)
 PIECES = {"A1": A1, "A2": A2, "B1": B1, "B2": B2}
 
 
@@ -64,7 +66,7 @@
     dq_out, dk_out, dv_out, np_out, phi_out, halo_out,
     ke_ref, ve_ref, kc_v, vc_v, k_st, v_st, qh, kh, vh, kt, vt, do_all, w_f, ps_f, w_t,
     pt, at, gw, dk_acc, dv_acc, dq_st, dk_st, dv_st, phi_f, phi_b,
-    load_sem, own_sem, out_sem, a2a_s, a2a_r, ag_s, ag_r, back_s, back_r, halo_s, halo_r,
+    load_sem, own_sem, out_sem, a2a_s, a2a_r, ag_s, ag_r, back_s, back_r, halo_s, halo_r, turn,
 ):
     me = lax.axis_index("seq")
     agent = lax.axis_index("agent")
@@ -104,9 +106,29 @@
     nxt, prv = lax.rem(agent + 1, N_AGENT), lax.rem(agent + N_AGENT - 1, N_AGENT)
     for other in (nxt, prv):
         pl.semaphore_signal(barrier, inc=1, device_id={"agent": other}, device_id_type=MESH)
+    def scaled(codes, expo, out):
+        factor = jnp.exp2(expo[...].astype(jnp.float32))
+        for h in range(HEADS):
+            c = slice(h * HDIM, (h + 1) * HDIM)
+            out[:, c] = (codes[:, c].astype(jnp.float32) * factor[0:1, h : h + 1]).astype(
+                jnp.bfloat16
+            )
+
+    for codes, expo, out, a, b in (
+        (kc_v, ke_ref, k_st, "ke", "k"),
+        (vc_v, ve_ref, v_st, "ve", "v"),
+    ):
+        loads[a].wait()
+        loads[b].wait()
+        scaled(codes, expo, out)
     pl.semaphore_wait(barrier, len(peers) + 2)
 
     sent = []
+
+    place = lax.rem(agent, 8)
+    ends = jnp.logical_or(place == 0, place == 7)
+    mates = jnp.logical_or(place == 1, place == 6)
+    mate = agent + 1 - 2 * lax.rem(agent, 2)
 
     def push(src, dst, ssem, rsem, target):
         copy = pltpu.make_async_remote_copy(
@@ -134,22 +156,8 @@
             if r:
                 arrived(dst.at[rows(at_rel(-dy, dx)), :], a2a_r.at[j, r], a2a_s.at[j, r])
 
-    def scaled(codes, expo, out):
-        factor = jnp.exp2(expo[...].astype(jnp.float32))
-        for h in range(HEADS):
-            c = slice(h * HDIM, (h + 1) * HDIM)
-            out[:, c] = (codes[:, c].astype(jnp.float32) * factor[0:1, h : h + 1]).astype(
-                jnp.bfloat16
-            )
-
     a2a_send(0, q_hbm, qh)
-    loads["ke"].wait()
-    loads["k"].wait()
-    scaled(kc_v, ke_ref, k_st)
     a2a_send(1, k_st, kh)
-    loads["ve"].wait()
-    loads["v"].wait()
-    scaled(vc_v, ve_ref, v_st)
     a2a_send(2, v_st, vh)
 
     step = {"xp": (0, 1), "up": (1, 0), "dn": (-1, 0)}
@@ -171,6 +179,10 @@
         _, _, (dy, dx), piece = MSGS[kind]
         first, width = PIECES[piece]
         arrived(do_all.at[rows(at_rel(dy, dx)), pl.ds(first, width)], ag_r.at[kind], ag_s.at[kind])
+
+    @pl.when(mates)
+    def _():
+        pl.semaphore_wait(turn, 1)
 
     for name in ("PB1", "MB2", "XA1", "PB2", "MB1", "XA2", "PA1", "MA2", "PA2", "MA1", "XB1", "XB2"):
         ag_send(name, own=True)
@@ -243,7 +255,15 @@
         pair = pair_of(dy)
         gw[...] += nn(at[pair], do_all[prows(pair), :])
 
-    def backward(dy):
+    def send_rows(j, st, out, dy):
+        for dx in range(2):
+            r = (dy % 4) * 2 + dx
+            t = at_rel(dy, dx)
+            if r:
+                push(st.at[rows(t), :], out.at[:, cols(me)], back_s.at[j, r], back_r.at[j, r],
+                     {"seq": t})
+
+    def backward(dy, last=False):
         pair = pair_of(dy)
         q = qh[prows(pair), :]
         d_f = nn(do_all[prows(pair), :], w_t[...])
@@ -251,23 +271,32 @@
         d_t = d_b.astype(jnp.float32).T
         row_dot = jnp.sum(d_t * at[pair].astype(jnp.float32), axis=0, keepdims=True)
         prob = pt[pair]
+        if last:
+            dv_st[...] = (dv_acc[...] + nn(prob.astype(jnp.bfloat16), d_b)).astype(jnp.bfloat16)
+            for away in (2, 1, -1, 0):
+                send_rows(2, dv_st, dv_out, away)
+        else:
+            dv_acc[...] += nn(prob.astype(jnp.bfloat16), d_b)
         d_s = (prob * (nt(vh[...], d_b) - row_dot) * SCALE).astype(jnp.bfloat16)
-        dk_acc[...] += nn(d_s, q)
-        dv_acc[...] += nn(prob.astype(jnp.bfloat16), d_b)
+        if last:
+            dk_st[...] = (dk_acc[...] + nn(d_s, q)).astype(jnp.bfloat16)
+            for away in (2, 1, -1, 0):
+                send_rows(1, dk_st, dk_out, away)
+        else:
+            dk_acc[...] += nn(d_s, q)
         dq_st[prows(pair), :] = nn(kt[...], d_s).T.astype(jnp.bfloat16)
-
-    def send_rows(j, st, out, dy):
-        for dx in range(2):
-            r = (dy % 4) * 2 + dx
-            t = at_rel(dy, dx)
-            if r:
-                push(st.at[rows(t), :], out.at[:, cols(me)], back_s.at[j, r], back_r.at[j, r],
-                     {"seq": t})
+        if last:
+            send_rows(0, dq_st, dq_out, 2)
 
     outs = ((dq_st, dq_out), (dk_st, dk_out), (dv_st, dv_out))
 
     stage_b()
     stage_x()
+
+    @pl.when(ends)
+    def _():
+        pl.semaphore_signal(turn, inc=1, device_id={"agent": mate}, device_id_type=MESH)
+
     own_k.wait()
     own_v.wait()
     loads["q"].wait()
@@ -285,6 +314,8 @@
     forward(3)
 
     loads["d"].wait()
+    loads["p"].wait()
+    ps_f[...] = 2.0 * w_f[...] - ps_f[...]
     ag_wait("XB1")
     ag_wait("XB2")
     add_grad(0)
@@ -305,37 +336,36 @@
 
     for name in ("P2A1", "M2A2", "P2XA1", "M2XA2", "XP2B1", "XM2B2"):
         ag_wait(name)
-    add_grad(2)
-
-    loads["p"].wait()
-    new_psi = w_f[...] - 0.02 * gw[...]
-    phi = new_psi + w_f[...] - ps_f[...]
-    phi_b[...] = phi.astype(jnp.bfloat16)
-    for i, other in enumerate((nxt, prv)):
-        push(phi_b, halo_out.at[i], halo_s.at[i], halo_r.at[i], {"agent": other})
-    gw[...] = new_psi
-    phi_f[...] = phi
+    last = pair_of(2)
+    for half in range(2):
+        for c in range(half * D // 2, (half + 1) * D // 2, 256):
+            g = gw[:, c : c + 256] + nn(at[last], do_all[prows(last), c : c + 256])
+            gw[:, c : c + 256] = g
+            phi = ps_f[:, c : c + 256] - 0.02 * g
+            phi_f[:, c : c + 256] = phi
+            phi_b[:, c : c + 256] = phi.astype(jnp.bfloat16)
+        part = pl.ds(half * D // 2, D // 2)
+        for i, other in enumerate((nxt, prv)):
+            push(phi_b.at[:, part], halo_out.at[i, :, part], halo_s.at[i, half], halo_r.at[i, half],
+                 {"agent": other})
+
+    backward(2, last=True)
+    gw[...] = w_f[...] - 0.02 * gw[...]
     stores = [
         pltpu.make_async_copy(gw, np_out, out_sem.at[0]),
         pltpu.make_async_copy(phi_f, phi_out, out_sem.at[1]),
     ]
     for copy in stores:
         copy.start()
-
-    backward(2)
-    dk_st[...] = dk_acc[...].astype(jnp.bfloat16)
-    dv_st[...] = dv_acc[...].astype(jnp.bfloat16)
-    for dy in (2, 1, -1, 0):
-        send_rows(1, dk_st, dk_out, dy)
-        send_rows(2, dv_st, dv_out, dy)
-    send_rows(0, dq_st, dq_out, 2)
     own = []
     for j, (st, out) in enumerate(outs):
         own.append(pltpu.make_async_copy(st.at[rows(me), :], out.at[:, cols(me)], own_sem.at[2 + j]))
         own[-1].start()
 
-    for i in range(2):
-        arrived(halo_out.at[i], halo_r.at[i], halo_s.at[i])
+    for half in range(2):
+        part = pl.ds(half * D // 2, D // 2)
+        for i in range(2):
+            arrived(halo_out.at[i, :, part], halo_r.at[i, half], halo_s.at[i, half])
     for copy in stores:
         copy.wait()
     for j, (st, out) in enumerate(outs):
@@ -349,33 +379,53 @@
 
 def finish(
     mix_hbm, dq, dk, dv, psi, phi, halo, dq_out, dk_out, dv_out, nw_out, np_out,
-    mix, phi_v, halo_v, load_sem, sem,
+    mix, dq_v, dk_v, dv_v, psi_v, phi_v, halo_v, load_sem, phi_sem, sem, nw_sem,
 ):
-    loads = [
-        pltpu.make_async_copy(a, b, load_sem.at[i])
-        for i, (a, b) in enumerate(((mix_hbm, mix), (phi, phi_v), (halo, halo_v)))
-    ]
-    for copy in loads:
-        copy.start()
-    copies = [
-        pltpu.make_async_copy(a, b, sem.at[i])
-        for i, (a, b) in enumerate(((psi, np_out), (dq, dq_out), (dk, dk_out), (dv, dv_out)))
-    ]
-    for copy in copies:
-        copy.start()
-    for copy in loads:
-        copy.wait()
+    mix_load = pltpu.make_async_copy(mix_hbm, mix, load_sem.at[0])
+    mix_load.start()
+    chunks = []
+    for c in range(N_CHUNK):
+        r = pl.ds(c * CHUNK, CHUNK)
+        chunks.append(
+            (
+                pltpu.make_async_copy(phi.at[r, :], phi_v.at[r, :], phi_sem.at[0, c]),
+                pltpu.make_async_copy(halo.at[:, r, :], halo_v.at[:, r, :], phi_sem.at[1, c]),
+                pltpu.make_async_copy(phi_v.at[r, :], nw_out.at[r, :], nw_sem.at[c]),
+            )
+        )
+        chunks[-1][0].start()
+        chunks[-1][1].start()
+    rest = []
+    for i, (a, b, out) in enumerate(
+        ((psi, psi_v, np_out), (dq, dq_v, dq_out), (dk, dk_v, dk_out), (dv, dv_v, dv_out))
+    ):
+        rest.append(
+            (
+                pltpu.make_async_copy(a, b, load_sem.at[i + 1]),
+                pltpu.make_async_copy(b, out, sem.at[i]),
+            )
+        )
+        rest[-1][0].start()
+    mix_load.wait()
     before = mix[0, 0].astype(jnp.float32)
     after = mix[0, 1].astype(jnp.float32)
-    phi_v[...] = (
-        (16.0 - before - after) * phi_v[...]
-        + before * halo_v[0].astype(jnp.float32)
-        + after * halo_v[1].astype(jnp.float32)
-    ) * 0.0625
-    copies.append(pltpu.make_async_copy(phi_v, nw_out, sem.at[4]))
-    copies[-1].start()
-    for copy in copies:
-        copy.wait()
+    for c, (own, others, store) in enumerate(chunks):
+        r = slice(c * CHUNK, (c + 1) * CHUNK)
+        own.wait()
+        others.wait()
+        phi_v[r, :] = (
+            (16.0 - before - after) * phi_v[r, :]
+            + before * halo_v[0, r, :].astype(jnp.float32)
+            + after * halo_v[1, r, :].astype(jnp.float32)
+        ) * 0.0625
+        store.start()
+    for load, store in rest:
+        load.wait()
+        store.start()
+    for _, _, store in chunks:
+        store.wait()
+    for _, store in rest:
+        store.wait()
 
 
 def local(
@@ -424,8 +474,9 @@
             pltpu.SemaphoreType.DMA((N_MSG,)),
             pltpu.SemaphoreType.DMA((3, N_SEQ)),
             pltpu.SemaphoreType.DMA((3, N_SEQ)),
-            pltpu.SemaphoreType.DMA((2,)),
-            pltpu.SemaphoreType.DMA((2,)),
+            pltpu.SemaphoreType.DMA((2, 2)),
+            pltpu.SemaphoreType.DMA((2, 2)),
+            pltpu.SemaphoreType.REGULAR,
         ],
         compiler_params=pltpu.CompilerParams(
             collective_id=0, has_side_effects=True, vmem_limit_bytes=VMEM
@@ -447,10 +498,16 @@
         out_specs=[hbm] * 5,
         scratch_shapes=[
             pltpu.SMEM((1, 2), jnp.int32),
+            pltpu.VMEM((TOK, HD), bf),
+            pltpu.VMEM((TOK, HD), bf),
+            pltpu.VMEM((TOK, HD), bf),
+            pltpu.VMEM((HDIM, D), f32),
             pltpu.VMEM((HDIM, D), f32),
             pltpu.VMEM((2, HDIM, D), bf),
-            pltpu.SemaphoreType.DMA((3,)),
             pltpu.SemaphoreType.DMA((5,)),
+            pltpu.SemaphoreType.DMA((2, N_CHUNK)),
+            pltpu.SemaphoreType.DMA((4,)),
+            pltpu.SemaphoreType.DMA((N_CHUNK,)),
         ],
         compiler_params=pltpu.CompilerParams(vmem_limit_bytes=VMEM),
         name="finish",

time: 117 us -> 60.7 us (0.52)
  the two profiles are of different devices: /device:TPU:0 before, /device:TPU:1 now
where the time goes in v3:
time: 60.7 us; the launch traced here: 60.6 us
  Pallas kernels  59.9 us (99%)
  between operations  0.64 us (1%)
    pallas_call x1, Pallas kernels, local(): pl.pallas_call(kernel, out_shape=[small] * 3 + [large] * 2 + [jax.ShapeDt...  56.4 us
    pallas_call x1, Pallas kernels, local(): pl.pallas_call(finish, out_shape=[small] * 3 + [large] * 2, in_specs=[hbm...  3.54 us

profile of v3, /device:TPU:1, one launch (start us, length us, event | category | flops | bytes accessed | tf_op | source)
XLA Modules:
  0.0 60.6 jit_solution(9148912308000612187)
XLA Ops:
  0.6 56.4 %exact_diffusion_step.1 = (bf16[128,1024]{1,0:T(8,128)(2,1)}, bf16[128,1024]{1,0:T(8,128)(2,1)}, bf16[128,1024]{1,0:T(8,128)(2,1)}, f32[128,2048]{1,0:T(8,128)},...) custom-call(s32[1,8]{1,0:T(1,128)} %bitcast.24, s32[1,8]{1,0:T(1,128)} %bitcast.25, bf16[128,1024]{1,0:T(8,128)(2,1)} %bitcast.18, ...), custom_call_target="tpu_custom_call" | custom-call | flops 2684354560 | bytes 8388608 | tf_op jit(solution)/shard_map/exact_diffusion_step/pallas_call | solution.py:437
  57.0 3.5 %finish.1 = (bf16[128,1024]{1,0:T(8,128)(2,1)}, bf16[128,1024]{1,0:T(8,128)(2,1)}, bf16[128,1024]{1,0:T(8,128)(2,1)}, f32[128,2048]{1,0:T(8,128)}, f32[128,2048]{1,0:T(8,128)}) custom-call(s32[1,2]{1,0:T(1,128)} %mix_hbm.1, bf16[128,1024]{1,0:T(8,128)(2,1)} %get-tuple-element.16.dq, bf16[128,1024]{1,0:T(8,128)(2,1)} %get-tuple-element.17.dk, ...), custom_call_target="tpu_custom_call" | custom-call | tf_op jit(solution)/shard_map/finish/pallas_call | solution.py:494

commit v4 on v3

--- a/solution.py
+++ b/solution.py
@@ -14,10 +14,7 @@
 HD = HEADS * HDIM
 D = 2048
 PAIR = 2 * TOK
-N_PAIR = TOKENS // PAIR
 VMEM = 62 * 1024 * 1024
-CHUNK = 32
-N_CHUNK = HDIM // CHUNK
 SCALE = HDIM ** (-0.5)
 MESH = pl.DeviceIdType.MESH
 
@@ -51,6 +48,7 @@
 MSGS = _gather_messages()
 KIND = {m[0]: i for i, m in enumerate(MSGS)}
 N_MSG = len(MSGS)
+LAST = (("XP2B1", "B1"), ("XM2B2", "B2"), ("P2XA1", "A1"), ("M2XA2", "A2"))
 
 
 def nt(a, b):
@@ -62,10 +60,10 @@
 
 
 def kernel(
-    ke_hbm, ve_hbm, q_hbm, kc_hbm, vc_hbm, do_hbm, w_hbm, ps_hbm,
-    dq_out, dk_out, dv_out, np_out, phi_out, halo_out,
-    ke_ref, ve_ref, kc_v, vc_v, k_st, v_st, qh, kh, vh, kt, vt, do_all, w_f, ps_f, w_t,
-    pt, at, gw, dk_acc, dv_acc, dq_st, dk_st, dv_st, phi_f, phi_b,
+    mix_hbm, ke_hbm, ve_hbm, q_hbm, kc_hbm, vc_hbm, do_hbm, w_hbm, ps_hbm,
+    dq_out, dk_out, dv_out, nw_out, np_out,
+    mix_ref, ke_ref, ve_ref, kc_v, vc_v, k_st, v_st, qh, kh, vh, kt, vt, do_all, w_f, ps_f, w_t,
+    pt, at, gw, dk_acc, dv_acc, dq_st, dk_st, dv_st, phi_f, phi_b, halo,
     load_sem, own_sem, out_sem, a2a_s, a2a_r, ag_s, ag_r, back_s, back_r, halo_s, halo_r, turn,
 ):
     me = lax.axis_index("seq")
@@ -95,6 +93,7 @@
             ("w", w_hbm, w_f),
             ("d", do_hbm, do_all.at[rows(me), :]),
             ("p", ps_hbm, ps_f),
+            ("m", mix_hbm, mix_ref),
         )
     ):
         loads[name] = pltpu.make_async_copy(src, dst, load_sem.at[i])
@@ -174,11 +173,13 @@
         src = do_hbm.at[:, pl.ds(first, width)] if own else here
         push(src, here, ag_s.at[kind], ag_r.at[kind], {"seq": at_rel(ty, tx)})
 
-    def ag_wait(name):
-        kind = KIND[name]
-        _, _, (dy, dx), piece = MSGS[kind]
-        first, width = PIECES[piece]
-        arrived(do_all.at[rows(at_rel(dy, dx)), pl.ds(first, width)], ag_r.at[kind], ag_s.at[kind])
+    def ag_wait(*names):
+        for name in names:
+            kind = KIND[name]
+            _, _, (dy, dx), piece = MSGS[kind]
+            first, width = PIECES[piece]
+            here = do_all.at[rows(at_rel(dy, dx)), pl.ds(first, width)]
+            arrived(here, ag_r.at[kind], ag_s.at[kind])
 
     @pl.when(mates)
     def _():
@@ -199,61 +200,54 @@
     dv_acc[...] = jnp.zeros_like(dv_acc)
     gw[...] = jnp.zeros_like(gw)
 
+    def pass_on(arrives, *then):
+        ag_wait(arrives)
+        for name in then:
+            ag_send(name)
+
     def stage_b():
-        ag_wait("PB1")
-        ag_send("P2B1")
-        ag_send("XPB1")
-        ag_wait("MB2")
-        ag_send("M2B2")
-        ag_send("XMB2")
-        ag_wait("PB2")
-        ag_send("XPB2")
-        ag_wait("MB1")
-        ag_send("XMB1")
+        pass_on("PB1", "P2B1", "XPB1")
+        pass_on("MB2", "M2B2", "XMB2")
+        pass_on("PB2", "XPB2")
+        pass_on("MB1", "XMB1")
 
     def stage_x():
-        ag_wait("XA1")
-        ag_send("PXA1")
-        ag_send("MXA1")
-        ag_wait("XA2")
-        ag_send("PXA2")
-        ag_send("MXA2")
+        pass_on("XA1", "PXA1", "MXA1")
+        pass_on("XA2", "PXA2", "MXA2")
 
     def stage_a():
-        ag_wait("PA1")
-        ag_send("P2A1")
-        ag_wait("MA2")
-        ag_send("M2A2")
+        pass_on("PA1", "P2A1")
+        pass_on("MA2", "M2A2")
 
     def stage_2b():
-        ag_wait("P2B1")
-        ag_send("XP2B1")
-        ag_wait("M2B2")
-        ag_send("XM2B2")
+        pass_on("P2B1", "XP2B1")
+        pass_on("M2B2", "XM2B2")
 
     def stage_xa():
-        ag_wait("PXA1")
-        ag_send("P2XA1")
-        ag_wait("MXA2")
-        ag_send("M2XA2")
+        pass_on("PXA1", "P2XA1")
+        pass_on("MXA2", "M2XA2")
 
     def forward(p):
         q = qh[p * PAIR : (p + 1) * PAIR, :]
         s = nt(kh[...], q) * SCALE
         e = jnp.exp(s - jnp.max(s, axis=0, keepdims=True))
         prob = e / jnp.sum(e, axis=0, keepdims=True)
-        pt[p] = prob
-        at[p] = nn(vt[...], prob.astype(jnp.bfloat16)).astype(jnp.bfloat16)
+        att = nn(vt[...], prob.astype(jnp.bfloat16)).astype(jnp.bfloat16)
+        for i in range(2):
+            pt[2 * p + i] = prob[:, i * TOK : (i + 1) * TOK]
+            at[2 * p + i] = att[:, i * TOK : (i + 1) * TOK]
+
+    def span(first, count):
+        return pl.ds(pl.multiple_of(first * TOK, TOK), count * TOK)
+
+    def beside(ref, first, count):
+        return jnp.concatenate([ref[first + i] for i in range(count)], axis=1)
 
     def pair_of(dy):
-        return lax.rem(y + (dy + 8), 4)
-
-    def prows(pair):
-        return pl.ds(pl.multiple_of(pair * PAIR, PAIR), PAIR)
-
-    def add_grad(dy):
-        pair = pair_of(dy)
-        gw[...] += nn(at[pair], do_all[prows(pair), :])
+        return lax.rem(y + (dy + 8), 4) * 2
+
+    def add_grad(first, count):
+        gw[...] += nn(beside(at, first, count), do_all[span(first, count), :])
 
     def send_rows(j, st, out, dy):
         for dx in range(2):
@@ -263,14 +257,14 @@
                 push(st.at[rows(t), :], out.at[:, cols(me)], back_s.at[j, r], back_r.at[j, r],
                      {"seq": t})
 
-    def backward(dy, last=False):
-        pair = pair_of(dy)
-        q = qh[prows(pair), :]
-        d_f = nn(do_all[prows(pair), :], w_t[...])
-        d_b = d_f.astype(jnp.bfloat16)
+    def backward(first, count, last=False):
+        here = span(first, count)
+        q = qh[here, :]
+        d_b = nn(do_all[here, :], w_t[...]).astype(jnp.bfloat16)
         d_t = d_b.astype(jnp.float32).T
-        row_dot = jnp.sum(d_t * at[pair].astype(jnp.float32), axis=0, keepdims=True)
-        prob = pt[pair]
+        att = beside(at, first, count).astype(jnp.float32)
+        row_dot = jnp.sum(d_t * att, axis=0, keepdims=True)
+        prob = beside(pt, first, count)
         if last:
             dv_st[...] = (dv_acc[...] + nn(prob.astype(jnp.bfloat16), d_b)).astype(jnp.bfloat16)
             for away in (2, 1, -1, 0):
@@ -284,7 +278,7 @@
                 send_rows(1, dk_st, dk_out, away)
         else:
             dk_acc[...] += nn(d_s, q)
-        dq_st[prows(pair), :] = nn(kt[...], d_s).T.astype(jnp.bfloat16)
+        dq_st[here, :] = nn(kt[...], d_s).T.astype(jnp.bfloat16)
         if last:
             send_rows(0, dq_st, dq_out, 2)
 
@@ -316,116 +310,90 @@
     loads["d"].wait()
     loads["p"].wait()
     ps_f[...] = 2.0 * w_f[...] - ps_f[...]
-    ag_wait("XB1")
-    ag_wait("XB2")
-    add_grad(0)
-    backward(0)
+    ag_wait("XB1", "XB2")
+    add_grad(pair_of(0), 2)
+    backward(pair_of(0), 2)
     send_rows(0, dq_st, dq_out, 0)
 
-    for name in ("PA2", "PXA2", "XPB1", "XPB2"):
+    ag_wait("PA2", "PXA2", "XPB1", "XPB2")
+    add_grad(pair_of(-1), 2)
+    backward(pair_of(-1), 2)
+    send_rows(0, dq_st, dq_out, -1)
+
+    ag_wait("MA1", "MXA1", "XMB1", "XMB2")
+    add_grad(pair_of(1), 2)
+    backward(pair_of(1), 2)
+    send_rows(0, dq_st, dq_out, 1)
+
+    ag_wait("P2A1", "M2A2")
+    add_grad(at_rel(2, 0), 1)
+    backward(at_rel(2, 0), 1)
+
+    last = at_rel(2, 1)
+    for n, (name, piece) in enumerate(LAST):
         ag_wait(name)
-    add_grad(-1)
-    backward(-1)
-    send_rows(0, dq_st, dq_out, -1)
-
-    for name in ("MA1", "MXA1", "XMB1", "XMB2"):
-        ag_wait(name)
-    add_grad(1)
-    backward(1)
-    send_rows(0, dq_st, dq_out, 1)
-
-    for name in ("P2A1", "M2A2", "P2XA1", "M2XA2", "XP2B1", "XM2B2"):
-        ag_wait(name)
-    last = pair_of(2)
-    for half in range(2):
-        for c in range(half * D // 2, (half + 1) * D // 2, 256):
-            g = gw[:, c : c + 256] + nn(at[last], do_all[prows(last), c : c + 256])
-            gw[:, c : c + 256] = g
-            phi = ps_f[:, c : c + 256] - 0.02 * g
-            phi_f[:, c : c + 256] = phi
-            phi_b[:, c : c + 256] = phi.astype(jnp.bfloat16)
-        part = pl.ds(half * D // 2, D // 2)
+        first, width = PIECES[piece]
+        for c in range(first, first + width, 128):
+            g = gw[:, c : c + 128] + nn(at[last], do_all[rows(last), c : c + 128])
+            gw[:, c : c + 128] = g
+            phi = ps_f[:, c : c + 128] - 0.02 * g
+            phi_f[:, c : c + 128] = phi
+            phi_b[:, c : c + 128] = phi.astype(jnp.bfloat16)
+        part = pl.ds(first, width)
         for i, other in enumerate((nxt, prv)):
-            push(phi_b.at[:, part], halo_out.at[i, :, part], halo_s.at[i, half], halo_r.at[i, half],
+            push(phi_b.at[:, part], halo.at[i, :, part], halo_s.at[i, n], halo_r.at[i, n],
                  {"agent": other})
 
-    backward(2, last=True)
+    backward(last, 1, last=True)
     gw[...] = w_f[...] - 0.02 * gw[...]
-    stores = [
-        pltpu.make_async_copy(gw, np_out, out_sem.at[0]),
-        pltpu.make_async_copy(phi_f, phi_out, out_sem.at[1]),
-    ]
-    for copy in stores:
-        copy.start()
+    stores = [pltpu.make_async_copy(gw, np_out, out_sem.at[0])]
+    stores[0].start()
     own = []
     for j, (st, out) in enumerate(outs):
         own.append(pltpu.make_async_copy(st.at[rows(me), :], out.at[:, cols(me)], own_sem.at[2 + j]))
         own[-1].start()
 
-    for half in range(2):
-        part = pl.ds(half * D // 2, D // 2)
+    loads["m"].wait()
+    before = mix_ref[0, 0].astype(jnp.float32)
+    after = mix_ref[0, 1].astype(jnp.float32)
+    for n, (_, piece) in enumerate(LAST):
+        first, width = PIECES[piece]
+        part = pl.ds(first, width)
         for i in range(2):
-            arrived(halo_out.at[i, :, part], halo_r.at[i, half], halo_s.at[i, half])
-    for copy in stores:
-        copy.wait()
+            arrived(halo.at[i, :, part], halo_r.at[i, n], halo_s.at[i, n])
+        c = slice(first, first + width)
+        phi_f[:, c] = (
+            (16.0 - before - after) * phi_f[:, c]
+            + before * halo[0, :, c].astype(jnp.float32)
+            + after * halo[1, :, c].astype(jnp.float32)
+        ) * 0.0625
+        stores.append(
+            pltpu.make_async_copy(phi_f.at[:, part], nw_out.at[:, part], out_sem.at[1 + n])
+        )
+        stores[-1].start()
     for j, (st, out) in enumerate(outs):
         own[j].wait()
         for r, (dy, dx) in enumerate(rels):
             if r:
                 arrived(out.at[:, cols(at_rel(-dy, dx))], back_r.at[j, r], back_s.at[j, r])
+    for copy in stores:
+        copy.wait()
     for copy in sent:
         copy.wait_send()
 
 
-def finish(
-    mix_hbm, dq, dk, dv, psi, phi, halo, dq_out, dk_out, dv_out, nw_out, np_out,
-    mix, dq_v, dk_v, dv_v, psi_v, phi_v, halo_v, load_sem, phi_sem, sem, nw_sem,
-):
-    mix_load = pltpu.make_async_copy(mix_hbm, mix, load_sem.at[0])
-    mix_load.start()
-    chunks = []
-    for c in range(N_CHUNK):
-        r = pl.ds(c * CHUNK, CHUNK)
-        chunks.append(
-            (
-                pltpu.make_async_copy(phi.at[r, :], phi_v.at[r, :], phi_sem.at[0, c]),
-                pltpu.make_async_copy(halo.at[:, r, :], halo_v.at[:, r, :], phi_sem.at[1, c]),
-                pltpu.make_async_copy(phi_v.at[r, :], nw_out.at[r, :], nw_sem.at[c]),
-            )
-        )
-        chunks[-1][0].start()
-        chunks[-1][1].start()
-    rest = []
-    for i, (a, b, out) in enumerate(
-        ((psi, psi_v, np_out), (dq, dq_v, dq_out), (dk, dk_v, dk_out), (dv, dv_v, dv_out))
-    ):
-        rest.append(
-            (
-                pltpu.make_async_copy(a, b, load_sem.at[i + 1]),
-                pltpu.make_async_copy(b, out, sem.at[i]),
-            )
-        )
-        rest[-1][0].start()
-    mix_load.wait()
-    before = mix[0, 0].astype(jnp.float32)
-    after = mix[0, 1].astype(jnp.float32)
-    for c, (own, others, store) in enumerate(chunks):
-        r = slice(c * CHUNK, (c + 1) * CHUNK)
-        own.wait()
-        others.wait()
-        phi_v[r, :] = (
-            (16.0 - before - after) * phi_v[r, :]
-            + before * halo_v[0, r, :].astype(jnp.float32)
-            + after * halo_v[1, r, :].astype(jnp.float32)
-        ) * 0.0625
-        store.start()
-    for load, store in rest:
+def store(*refs):
+    ins, outs, held, load_sem, store_sem = refs[:5], refs[5:10], refs[10:15], refs[15], refs[16]
+    loads, stores = [], []
+    for i in range(5):
+        loads.append(pltpu.make_async_copy(ins[i], held[i], load_sem.at[i]))
+        stores.append(pltpu.make_async_copy(held[i], outs[i], store_sem.at[i]))
+        loads[i].start()
+    for load, copy in zip(loads, stores):
         load.wait()
-        store.start()
-    for _, _, store in chunks:
-        store.wait()
-    for _, store in rest:
-        store.wait()
+        copy.start()
+    for copy in stores:
+        copy.wait()
 
 
 def local(
@@ -434,12 +402,13 @@
     bf, f32 = jnp.bfloat16, jnp.float32
     hbm = pl.BlockSpec(memory_space=pltpu.HBM)
     small, large = jax.ShapeDtypeStruct((TOK, HD), bf), jax.ShapeDtypeStruct((HDIM, D), f32)
-    *grads, psi, phi, halo = pl.pallas_call(
+    outs = pl.pallas_call(
         kernel,
-        out_shape=[small] * 3 + [large] * 2 + [jax.ShapeDtypeStruct((2, HDIM, D), bf)],
-        in_specs=[hbm] * 8,
-        out_specs=[hbm] * 6,
+        out_shape=[small] * 3 + [large] * 2,
+        in_specs=[hbm] * 9,
+        out_specs=[hbm] * 5,
         scratch_shapes=[
+            pltpu.SMEM((1, 2), jnp.int32),
             pltpu.VMEM((1, HEADS), jnp.int32),
             pltpu.VMEM((1, HEADS), jnp.int32),
             pltpu.VMEM((TOK, HD), bf),
@@ -455,8 +424,8 @@
             pltpu.VMEM((HDIM, D), f32),
             pltpu.VMEM((HDIM, D), f32),
             pltpu.VMEM((D, HDIM), bf),
-            pltpu.VMEM((N_PAIR, TOKENS, PAIR), f32),
-            pltpu.VMEM((N_PAIR, HDIM, PAIR), bf),
+            pltpu.VMEM((N_SEQ, TOKENS, TOK), f32),
+            pltpu.VMEM((N_SEQ, HDIM, TOK), bf),
             pltpu.VMEM((HDIM, D), f32),
             pltpu.VMEM((TOKENS, HDIM), f32),
             pltpu.VMEM((TOKENS, HDIM), f32),
@@ -465,17 +434,18 @@
             pltpu.VMEM((TOKENS, HDIM), bf),
             pltpu.VMEM((HDIM, D), f32),
             pltpu.VMEM((HDIM, D), bf),
-            pltpu.SemaphoreType.DMA((8,)),
+            pltpu.VMEM((2, HDIM, D), bf),
+            pltpu.SemaphoreType.DMA((9,)),
             pltpu.SemaphoreType.DMA((5,)),
-            pltpu.SemaphoreType.DMA((2,)),
+            pltpu.SemaphoreType.DMA((1 + len(LAST),)),
             pltpu.SemaphoreType.DMA((3, N_SEQ)),
             pltpu.SemaphoreType.DMA((3, N_SEQ)),
             pltpu.SemaphoreType.DMA((N_MSG,)),
             pltpu.SemaphoreType.DMA((N_MSG,)),
             pltpu.SemaphoreType.DMA((3, N_SEQ)),
             pltpu.SemaphoreType.DMA((3, N_SEQ)),
-            pltpu.SemaphoreType.DMA((2, 2)),
-            pltpu.SemaphoreType.DMA((2, 2)),
+            pltpu.SemaphoreType.DMA((2, len(LAST))),
+            pltpu.SemaphoreType.DMA((2, len(LAST))),
             pltpu.SemaphoreType.REGULAR,
         ],
         compiler_params=pltpu.CompilerParams(
@@ -488,30 +458,20 @@
         ),
         name="exact_diffusion_step",
     )(
-        key_exps[0], value_exps[0], queries[0], key_codes[0], value_codes[0],
+        mixing, key_exps[0], value_exps[0], queries[0], key_codes[0], value_codes[0],
         d_out[0], out_weight[0], prev_psi[0],
     )
     outs = pl.pallas_call(
-        finish,
+        store,
         out_shape=[small] * 3 + [large] * 2,
-        in_specs=[hbm] * 7,
+        in_specs=[hbm] * 5,
         out_specs=[hbm] * 5,
-        scratch_shapes=[
-            pltpu.SMEM((1, 2), jnp.int32),
-            pltpu.VMEM((TOK, HD), bf),
-            pltpu.VMEM((TOK, HD), bf),
-            pltpu.VMEM((TOK, HD), bf),
-            pltpu.VMEM((HDIM, D), f32),
-            pltpu.VMEM((HDIM, D), f32),
-            pltpu.VMEM((2, HDIM, D), bf),
-            pltpu.SemaphoreType.DMA((5,)),
-            pltpu.SemaphoreType.DMA((2, N_CHUNK)),
-            pltpu.SemaphoreType.DMA((4,)),
-            pltpu.SemaphoreType.DMA((N_CHUNK,)),
-        ],
+        scratch_shapes=[pltpu.VMEM((TOK, HD), bf)] * 3
+        + [pltpu.VMEM((HDIM, D), f32)] * 2
+        + [pltpu.SemaphoreType.DMA((5,))] * 2,
         compiler_params=pltpu.CompilerParams(vmem_limit_bytes=VMEM),
         name="finish",
-    )(mixing, *grads, psi, phi, halo)
+    )(*outs)
     return tuple(out[None] for out in outs)
 
 

time: 60.7 us -> 60.2 us (level)
  no operation moved by 1% of the time
where the time goes in v4:
time: 60.2 us; the launch traced here: 60 us
  Pallas kernels  59.4 us (99%)
  between operations  0.64 us (1%)
    pallas_call x1, Pallas kernels, local(): pl.pallas_call(kernel, out_shape=[small] * 3 + [large] * 2, in_specs=[hbm...  56.5 us
    pallas_call x1, Pallas kernels, local(): pl.pallas_call(store, out_shape=[small] * 3 + [large] * 2, in_specs=[hbm]...  2.87 us

profile of v4, /device:TPU:1, one launch (start us, length us, event | category | flops | bytes accessed | tf_op | source)
XLA Modules:
  0.0 60.0 jit_solution(4502663239664611321)
XLA Ops:
  0.6 56.5 %exact_diffusion_step.1 = (bf16[128,1024]{1,0:T(8,128)(2,1)}, bf16[128,1024]{1,0:T(8,128)(2,1)}, bf16[128,1024]{1,0:T(8,128)(2,1)}, f32[128,2048]{1,0:T(8,128)}, f32[128,2048]{1,0:T(8,128)}) custom-call(s32[1,2]{1,0:T(1,128)} %mix_hbm.1, s32[1,8]{1,0:T(1,128)} %bitcast.24, s32[1,8]{1,0:T(1,128)} %bitcast.25, bf16[128,1024]{1,0:T(8,128)(2,1)} %bitcast.18, ...), custom_call_target="tpu_custom_call" | custom-call | flops 2684354560 | bytes 8388608 | tf_op jit(solution)/shard_map/exact_diffusion_step/pallas_call | solution.py:405
  57.1 2.9 %finish.1 = (bf16[128,1024]{1,0:T(8,128)(2,1)}, bf16[128,1024]{1,0:T(8,128)(2,1)}, bf16[128,1024]{1,0:T(8,128)(2,1)}, f32[128,2048]{1,0:T(8,128)}, f32[128,2048]{1,0:T(8,128)}) custom-call(bf16[128,1024]{1,0:T(8,128)(2,1)} %get-tuple-element.15.refs_0_, bf16[128,1024]{1,0:T(8,128)(2,1)} %get-tuple-element.16.refs_1_, ...), custom_call_target="tpu_custom_call" | custom-call | tf_op jit(solution)/shard_map/finish/pallas_call | solution.py:464

commit v5 on v4

--- a/solution.py
+++ b/solution.py
@@ -62,7 +62,7 @@
 def kernel(
     mix_hbm, ke_hbm, ve_hbm, q_hbm, kc_hbm, vc_hbm, do_hbm, w_hbm, ps_hbm,
     dq_out, dk_out, dv_out, nw_out, np_out,
-    mix_ref, ke_ref, ve_ref, kc_v, vc_v, k_st, v_st, qh, kh, vh, kt, vt, do_all, w_f, ps_f, w_t,
+    mix_ref, ke_ref, ve_ref, kc_v, vc_v, kv_st, qh, kvh, kt, vt, do_all, w_f, ps_f, w_t,
     pt, at, gw, dk_acc, dv_acc, dq_st, dk_st, dv_st, phi_f, phi_b, halo,
     load_sem, own_sem, out_sem, a2a_s, a2a_r, ag_s, ag_r, back_s, back_r, halo_s, halo_r, turn,
 ):
@@ -82,6 +82,12 @@
     rels = [(dy, dx) for dy in range(4) for dx in range(2)]
     peers = rels[1:]
 
+    barrier = pltpu.get_barrier_semaphore()
+    for dy, dx in peers:
+        pl.semaphore_signal(barrier, inc=1, device_id={"seq": at_rel(dy, dx)}, device_id_type=MESH)
+    nxt, prv = lax.rem(agent + 1, N_AGENT), lax.rem(agent + N_AGENT - 1, N_AGENT)
+    for other in (nxt, prv):
+        pl.semaphore_signal(barrier, inc=1, device_id={"agent": other}, device_id_type=MESH)
     loads = {}
     for i, (name, src, dst) in enumerate(
         (
@@ -99,23 +105,17 @@
         loads[name] = pltpu.make_async_copy(src, dst, load_sem.at[i])
         loads[name].start()
 
-    barrier = pltpu.get_barrier_semaphore()
-    for dy, dx in peers:
-        pl.semaphore_signal(barrier, inc=1, device_id={"seq": at_rel(dy, dx)}, device_id_type=MESH)
-    nxt, prv = lax.rem(agent + 1, N_AGENT), lax.rem(agent + N_AGENT - 1, N_AGENT)
-    for other in (nxt, prv):
-        pl.semaphore_signal(barrier, inc=1, device_id={"agent": other}, device_id_type=MESH)
     def scaled(codes, expo, out):
         factor = jnp.exp2(expo[...].astype(jnp.float32))
         for h in range(HEADS):
             c = slice(h * HDIM, (h + 1) * HDIM)
-            out[:, c] = (codes[:, c].astype(jnp.float32) * factor[0:1, h : h + 1]).astype(
+            kv_st[out, :, c] = (codes[:, c].astype(jnp.float32) * factor[0:1, h : h + 1]).astype(
                 jnp.bfloat16
             )
 
     for codes, expo, out, a, b in (
-        (kc_v, ke_ref, k_st, "ke", "k"),
-        (vc_v, ve_ref, v_st, "ve", "v"),
+        (kc_v, ke_ref, 0, "ke", "k"),
+        (vc_v, ve_ref, 1, "ve", "v"),
     ):
         loads[a].wait()
         loads[b].wait()
@@ -143,21 +143,22 @@
             device_id={"seq": at_rel(0, 1)}, device_id_type=MESH,
         ).wait_recv()
 
+    def rows_of(ref, block):
+        return ref.at[rows(block), :] if len(ref.shape) == 2 else ref.at[:, rows(block), :]
+
     def a2a_send(j, src, dst):
         for r, (dy, dx) in enumerate(rels):
             if r:
                 t = at_rel(dy, dx)
-                push(src.at[:, cols(t)], dst.at[rows(me), :], a2a_s.at[j, r], a2a_r.at[j, r],
-                     {"seq": t})
+                push(src.at[..., cols(t)], rows_of(dst, me), a2a_s.at[j, r], a2a_r.at[j, r], {"seq": t})
 
     def a2a_wait(j, dst):
         for r, (dy, dx) in enumerate(rels):
             if r:
-                arrived(dst.at[rows(at_rel(-dy, dx)), :], a2a_r.at[j, r], a2a_s.at[j, r])
+                arrived(rows_of(dst, at_rel(-dy, dx)), a2a_r.at[j, r], a2a_s.at[j, r])
 
     a2a_send(0, q_hbm, qh)
-    a2a_send(1, k_st, kh)
-    a2a_send(2, v_st, vh)
+    a2a_send(1, kv_st, kvh)
 
     step = {"xp": (0, 1), "up": (1, 0), "dn": (-1, 0)}
     back_to = {"xp": "xp", "up": "dn", "dn": "up"}
@@ -188,10 +189,8 @@
     for name in ("PB1", "MB2", "XA1", "PB2", "MB1", "XA2", "PA1", "MA2", "PA2", "MA1", "XB1", "XB2"):
         ag_send(name, own=True)
 
-    own_k = pltpu.make_async_copy(k_st.at[:, cols(me)], kh.at[rows(me), :], own_sem.at[0])
-    own_v = pltpu.make_async_copy(v_st.at[:, cols(me)], vh.at[rows(me), :], own_sem.at[1])
-    own_k.start()
-    own_v.start()
+    own_kv = pltpu.make_async_copy(kv_st.at[:, :, cols(me)], kvh.at[:, rows(me), :], own_sem.at[0])
+    own_kv.start()
 
     loads["w"].wait()
     for c in range(0, D, 256):
@@ -229,7 +228,7 @@
 
     def forward(p):
         q = qh[p * PAIR : (p + 1) * PAIR, :]
-        s = nt(kh[...], q) * SCALE
+        s = nt(kvh[0], q) * SCALE
         e = jnp.exp(s - jnp.max(s, axis=0, keepdims=True))
         prob = e / jnp.sum(e, axis=0, keepdims=True)
         att = nn(vt[...], prob.astype(jnp.bfloat16)).astype(jnp.bfloat16)
@@ -271,7 +270,7 @@
                 send_rows(2, dv_st, dv_out, away)
         else:
             dv_acc[...] += nn(prob.astype(jnp.bfloat16), d_b)
-        d_s = (prob * (nt(vh[...], d_b) - row_dot) * SCALE).astype(jnp.bfloat16)
+        d_s = (prob * (nt(kvh[1], d_b) - row_dot) * SCALE).astype(jnp.bfloat16)
         if last:
             dk_st[...] = (dk_acc[...] + nn(d_s, q)).astype(jnp.bfloat16)
             for away in (2, 1, -1, 0):
@@ -291,14 +290,12 @@
     def _():
         pl.semaphore_signal(turn, inc=1, device_id={"agent": mate}, device_id_type=MESH)
 
-    own_k.wait()
-    own_v.wait()
+    own_kv.wait()
     loads["q"].wait()
     a2a_wait(0, qh)
-    a2a_wait(1, kh)
-    a2a_wait(2, vh)
-    kt[...] = kh[...].astype(jnp.float32).T.astype(jnp.bfloat16)
-    vt[...] = vh[...].astype(jnp.float32).T.astype(jnp.bfloat16)
+    a2a_wait(1, kvh)
+    kt[...] = kvh[0].astype(jnp.float32).T.astype(jnp.bfloat16)
+    vt[...] = kvh[1].astype(jnp.float32).T.astype(jnp.bfloat16)
     forward(0)
     stage_a()
     forward(1)
@@ -344,10 +341,13 @@
             push(phi_b.at[:, part], halo.at[i, :, part], halo_s.at[i, n], halo_r.at[i, n],
                  {"agent": other})
 
+    early, sent[:] = sent[:], []
     backward(last, 1, last=True)
     gw[...] = w_f[...] - 0.02 * gw[...]
     stores = [pltpu.make_async_copy(gw, np_out, out_sem.at[0])]
     stores[0].start()
+    while early:
+        early.pop().wait_send()
     own = []
     for j, (st, out) in enumerate(outs):
         own.append(pltpu.make_async_copy(st.at[rows(me), :], out.at[:, cols(me)], own_sem.at[2 + j]))
@@ -371,7 +371,8 @@
             pltpu.make_async_copy(phi_f.at[:, part], nw_out.at[:, part], out_sem.at[1 + n])
         )
         stores[-1].start()
-    for j, (st, out) in enumerate(outs):
+    for j in (0, 2, 1):
+        _, out = outs[j]
         own[j].wait()
         for r, (dy, dx) in enumerate(rels):
             if r:
@@ -413,11 +414,9 @@
             pltpu.VMEM((1, HEADS), jnp.int32),
             pltpu.VMEM((TOK, HD), bf),
             pltpu.VMEM((TOK, HD), bf),
-            pltpu.VMEM((TOK, HD), bf),
-            pltpu.VMEM((TOK, HD), bf),
+            pltpu.VMEM((2, TOK, HD), bf),
             pltpu.VMEM((TOKENS, HDIM), bf),
-            pltpu.VMEM((TOKENS, HDIM), bf),
-            pltpu.VMEM((TOKENS, HDIM), bf),
+            pltpu.VMEM((2, TOKENS, HDIM), bf),
             pltpu.VMEM((HDIM, TOKENS), bf),
             pltpu.VMEM((HDIM, TOKENS), bf),
             pltpu.VMEM((TOKENS, D), bf),

time: 60.2 us -> 60.1 us (level)
  no operation moved by 1% of the time
where the time goes in v5:
time: 60.1 us; the launch traced here: 60 us
  Pallas kernels  59.4 us (99%)
  between operations  0.64 us (1%)
    pallas_call x1, Pallas kernels, local(): pl.pallas_call(kernel, out_shape=[small] * 3 + [large] * 2, in_specs=[hbm...  56.5 us
    pallas_call x1, Pallas kernels, local(): pl.pallas_call(store, out_shape=[small] * 3 + [large] * 2, in_specs=[hbm]...  2.87 us

profile of v5, /device:TPU:1, one launch (start us, length us, event | category | flops | bytes accessed | tf_op | source)
XLA Modules:
  0.0 60.0 jit_solution(6237284254988171232)
XLA Ops:
  0.6 56.5 %exact_diffusion_step.1 = (bf16[128,1024]{1,0:T(8,128)(2,1)}, bf16[128,1024]{1,0:T(8,128)(2,1)}, bf16[128,1024]{1,0:T(8,128)(2,1)}, f32[128,2048]{1,0:T(8,128)}, f32[128,2048]{1,0:T(8,128)}) custom-call(s32[1,2]{1,0:T(1,128)} %mix_hbm.1, s32[1,8]{1,0:T(1,128)} %bitcast.24, s32[1,8]{1,0:T(1,128)} %bitcast.25, bf16[128,1024]{1,0:T(8,128)(2,1)} %bitcast.18, ...), custom_call_target="tpu_custom_call" | custom-call | flops 2684354560 | bytes 8388608 | tf_op jit(solution)/shard_map/exact_diffusion_step/pallas_call | solution.py:406
  57.1 2.9 %finish.1 = (bf16[128,1024]{1,0:T(8,128)(2,1)}, bf16[128,1024]{1,0:T(8,128)(2,1)}, bf16[128,1024]{1,0:T(8,128)(2,1)}, f32[128,2048]{1,0:T(8,128)}, f32[128,2048]{1,0:T(8,128)}) custom-call(bf16[128,1024]{1,0:T(8,128)(2,1)} %get-tuple-element.15.refs_0_, bf16[128,1024]{1,0:T(8,128)(2,1)} %get-tuple-element.16.refs_1_, ...), custom_call_target="tpu_custom_call" | custom-call | tf_op jit(solution)/shard_map/finish/pallas_call | solution.py:463
